TPU v7x, 512 devices: a whole 4x8x8 slice. The times are simulated.
512 devices in a mesh: seq: 64 (over z, y_lo, core), head: 8 (over x, y_hi).
Axes of the slice: x: 4, y: 8 (y_hi: 2, y_lo: 4; y = y_hi * 4 + y_lo), z: 8, core: 2. Of those that a mesh axis runs over, the one named last changes fastest.
Arguments:
- queries: bfloat16 [2, 1024, 16384], P(None, 'seq', 'head'), may hold values from -80 to 80
- prefix_keys: bfloat16 [16384, 1024], P(('seq', 'head')), may hold values from -4 to 4
- prefix_values: bfloat16 [16384, 1024], P(('seq', 'head')), may hold values from -6 to 6
- cache_keys: bfloat16 [1024, 2, 1024], P('seq', None, 'head'), may hold values from -6 to 6
- cache_values: bfloat16 [1024, 2, 1024], P('seq', None, 'head'), may hold values from -6 to 6
- new_keys: bfloat16 [2, 1024, 1024], P(None, 'seq', 'head'), may hold values from -6 to 6
- new_values: bfloat16 [2, 1024, 1024], P(None, 'seq', 'head'), may hold values from -6 to 6
- suffix_len: int32 [1024], P('seq'), may hold values from 0 to 2
- out_weight: bfloat16 [16384, 16384], P('head', 'seq'), may hold values from -0.046875 to 0.046875
Outputs:
- projected: bfloat16 [2, 1024, 16384], P(None, 'head', 'seq')
Inputs may be any that keep to these rules, and one draw needn't show every extreme that they name: `suffix_len`: number of earlier suffix tokens of each completion; cache slots from it on are unused.
All inputs are finite; a program needn't handle non-finite values.
Results may differ from a plain program's by a relative error of at most 0.019.
Values may be sent and summed in bfloat16 or wider, within the bound.
No kernel may reach another device: no remote copies, remote signals or barrier semaphores. Data moves between devices by JAX's collectives and lax.ppermute only.
A program may use at most 64 MiB of HBM per device.

v0:
```python
import math

import jax
import jax.numpy as jnp
from jax import lax
from jax.sharding import PartitionSpec as P

QH = 128
KVH = 8
HD = 128
SUF = 2


def combine(first, second):
    row_max = jnp.maximum(first[0], second[0])
    left_factor = jnp.exp(first[0] - row_max)
    right_factor = jnp.exp(second[0] - row_max)
    total = first[1] * left_factor + second[1] * right_factor
    weighted = first[2] * left_factor[..., None] + second[2] * right_factor[..., None]
    return (row_max, total, weighted)


def block_partial(grouped, key_rows, value_rows):
    count = key_rows.shape[0]
    kv_heads = grouped.shape[2]
    keys_split = key_rows.reshape(count, kv_heads, HD)
    values_split = value_rows.reshape(count, kv_heads, HD)
    scores = jnp.einsum(
        "tbkgd,nkd->tbkgn", grouped, keys_split, preferred_element_type=jnp.float32
    ) * HD ** (-0.5)
    row_max = jnp.max(scores, axis=-1)
    weights = jnp.exp(scores - row_max[..., None])
    total = jnp.sum(weights, axis=-1)
    weighted = jnp.einsum(
        "tbkgn,nkd->tbkgd",
        weights.astype(jnp.bfloat16),
        values_split,
        preferred_element_type=jnp.float32,
    )
    return (row_max, total, weighted)


def prefix_partial(grouped, key_rows, value_rows):
    count = key_rows.shape[0]
    block_rows = math.gcd(count, 2048)
    block_count = count // block_rows
    key_blocks = key_rows.reshape(block_count, block_rows, key_rows.shape[1])
    value_blocks = value_rows.reshape(block_count, block_rows, value_rows.shape[1])
    start_state = block_partial(grouped, key_blocks[0], value_blocks[0])

    def advance(carry, blocks):
        return (combine(carry, block_partial(grouped, blocks[0], blocks[1])), None)

    result, unused = lax.scan(advance, start_state, (key_blocks[1:], value_blocks[1:]))
    return result


def suffix_partial(step_queries, cache_keys, cache_values, new_keys, new_values, suffix_len, step):
    local_rows = step_queries.shape[0]
    kv_heads = step_queries.shape[1]
    fresh_keys = jnp.swapaxes(new_keys[: step + 1], 0, 1).reshape(
        local_rows, step + 1, kv_heads, HD
    )
    fresh_values = jnp.swapaxes(new_values[: step + 1], 0, 1).reshape(
        local_rows, step + 1, kv_heads, HD
    )
    tail_keys = jnp.concatenate(
        [cache_keys.reshape(local_rows, SUF, kv_heads, HD), fresh_keys], axis=1
    )
    tail_values = jnp.concatenate(
        [cache_values.reshape(local_rows, SUF, kv_heads, HD), fresh_values], axis=1
    )
    slots = jnp.arange(SUF + step + 1, dtype=jnp.int32)
    valid = ((slots[None, :] < suffix_len[:, None]) | (slots[None, :] >= SUF))[:, None, None, :]
    scores = jnp.einsum(
        "bkgd,bjkd->bkgj", step_queries, tail_keys, preferred_element_type=jnp.float32
    ) * HD ** (-0.5)
    scores = jnp.where(valid, scores, jnp.float32(-1e30))
    row_max = jnp.max(scores, axis=-1)
    weights = jnp.where(valid, jnp.exp(scores - row_max[..., None]), jnp.float32(0.0))
    total = jnp.sum(weights, axis=-1)
    weighted = jnp.einsum(
        "bkgj,bjkd->bkgd",
        weights.astype(jnp.bfloat16),
        tail_values,
        preferred_element_type=jnp.float32,
    )
    return (row_max, total, weighted)


def per_device(
    queries,
    prefix_keys,
    prefix_values,
    cache_keys,
    cache_values,
    new_keys,
    new_values,
    suffix_len,
    out_weight,
):
    group_size = QH // KVH
    local_rows = queries.shape[1]
    kv_heads = cache_keys.shape[2] // HD
    grouped = queries.reshape(2, local_rows, kv_heads, group_size, HD)
    group_keys, group_values = (
        lax.all_to_all(prefix_keys, "head", split_axis=1, concat_axis=0, tiled=True),
        lax.all_to_all(prefix_values, "head", split_axis=1, concat_axis=0, tiled=True),
    )
    all_keys, all_values = (
        lax.all_gather(group_keys, "seq", axis=0, tiled=True),
        lax.all_gather(group_values, "seq", axis=0, tiled=True),
    )
    prompt_state = prefix_partial(grouped, all_keys, all_values)
    first_tail = suffix_partial(
        grouped[0], cache_keys, cache_values, new_keys, new_values, suffix_len, 0
    )
    second_tail = suffix_partial(
        grouped[1], cache_keys, cache_values, new_keys, new_values, suffix_len, 1
    )
    tail_state = tuple(
        (jnp.stack([first_tail[index], second_tail[index]], axis=0) for index in range(3))
    )
    merged = combine(prompt_state, tail_state)
    attended = (
        (merged[2] / merged[1][..., None])
        .astype(jnp.bfloat16)
        .reshape(2, local_rows, kv_heads * group_size * HD)
    )
    terms = jnp.einsum(
        "tbf,fd->tbd",
        lax.all_gather(attended, "seq", axis=1, tiled=True),
        out_weight,
        preferred_element_type=jnp.float32,
    )
    summed = lax.psum_scatter(terms.astype(jnp.bfloat16), "head", scatter_dimension=1, tiled=True)
    return summed


def solution(mesh):
    in_specs = (
        P(None, "seq", "head"),
        P(("seq", "head"), None),
        P(("seq", "head"), None),
        P("seq", None, "head"),
        P("seq", None, "head"),
        P(None, "seq", "head"),
        P(None, "seq", "head"),
        P("seq"),
        P("head", "seq"),
    )
    out_specs = P(None, "head", "seq")
    return jax.shard_map(
        per_device, mesh=mesh, in_specs=in_specs, out_specs=out_specs, check_vma=False
    )
```

profile of v0, /device:TPU:1, one launch (start us, length us, event | category | flops | bytes accessed | tf_op | source)
XLA Modules:
  0.0 532.0 jit_solution(172971231464517745)
XLA Ops:
  6.5 0.0 copy-start
  6.5 0.0 all-gather.4.cloned.1.call-start
  6.5 0.9 copy_bitcast_fusion.1
  7.5 19.2 %all_to_all.38 = bf16[32,8,128]{2,0,1:T(8,128)(2,1)} all-to-all(bf16[32,8,128]{2,0,1:T(8,128)(2,1)S(1)} %copy_bitcast_fusion.1), channel_id=1, replica_groups=mesh['seq'=64,'head'=8] {'head'}, dimensions={1} | all-to-all | bytes 131072 | tf_op jit(solution)/shard_map/all_to_all | solution.py:107
  26.7 0.0 all-gather.4.cloned.1.call-update
  26.7 0.0 all-gather.6.cloned.1.call-start
  26.8 0.9 copy_bitcast_fusion
  27.6 12.2 %all_to_all.39 = bf16[32,8,128]{2,0,1:T(8,128)(2,1)} all-to-all(bf16[32,8,128]{2,0,1:T(8,128)(2,1)S(1)} %copy_bitcast_fusion), channel_id=1, replica_groups=mesh['seq'=64,'head'=8] {'head'}, dimensions={1} | all-to-all | bytes 131072 | tf_op jit(solution)/shard_map/all_to_all | solution.py:108
  39.8 0.0 all-gather.6.cloned.1.call-update
  39.8 0.0 all-gather.8.cloned.1.call-start
  39.9 0.9 copy.28
  40.8 0.9 slice_bitcast_fusion.5
  41.7 0.7 copy.37
  42.4 0.7 slice_bitcast_fusion.7
  43.1 0.7 copy.36
  43.8 0.7 slice_bitcast_fusion.6
  44.6 0.7 fusion.78
  45.3 0.9 fusion.90
  46.1 0.1 fusion.54
  46.3 0.7 fusion.79
  47.0 0.9 fusion.89
  47.8 0.1 fusion.56
  48.0 1.2 convolution_bitcast_fusion.1
  49.1 1.1 convolution_bitcast_fusion
  50.2 95.6 %all-gather.4.cloned.1.call-done = bf16[16384,128]{1,0:T(8,128)(2,1)} async-done(((bf16[256,128]{1,0:T(8,128)(2,1)}), bf16[16384,128]{1,0:T(8,128)(2,1)}) %all-gather.4.cloned.1.call-update) | async-done | bytes 4194320 | tf_op jit(solution)/shard_map/all_gather | solution.py:111
  145.9 3.5 slice.46
  149.3 1.8 bitcast_reduce_fusion.1
  151.2 0.0 copy-start.1
  151.2 2.0 copy-done.1
  153.1 0.8 fusion.35
  153.9 112.8 %all-gather.6.cloned.1.call-done = bf16[16384,128]{1,0:T(8,128)(2,1)} async-done(((bf16[256,128]{1,0:T(8,128)(2,1)}), bf16[16384,128]{1,0:T(8,128)(2,1)}) %all-gather.6.cloned.1.call-update) | async-done | bytes 4194320 | tf_op jit(solution)/shard_map/all_gather | solution.py:112
  266.8 3.3 fusion.41
  270.0 0.3 copy-done.2
  270.4 1.9 slice.47
  272.3 32.8 %while.14 = (s32[]{:T(128)}, f32[2,16,1,16]{3,1,0,2:T(8,128)S(1)}, f32[2,16,1,16]{3,1,0,2:T(8,128)S(1)}, f32[2,16,1,16,128]{4,3,1,0,2:T(8,128)S(1)}, bf16[7,2048...) while((s32[]{:T(128)}, f32[2,16,1,16]{3,1,0,2:T(8,128)S(1)}, ...), condition=%wide.region_5.6_spmd, body=%wide.region_2.5_spmd.sunk | while | flops 545458688 | bytes 14326869 | solution.py:54
  272.3 1.8 bitcast_reduce_fusion.3
  274.1 0.8 fusion.105
  275.0 2.0 fusion.107
  277.0 1.8 bitcast_reduce_fusion.3
  278.8 0.8 fusion.105
  279.7 2.0 fusion.107
  281.6 1.8 bitcast_reduce_fusion.3
  283.5 0.8 fusion.105
  284.3 2.0 fusion.107
  286.3 1.8 bitcast_reduce_fusion.3
  288.2 0.8 fusion.105
  289.0 2.0 fusion.107
  291.0 1.8 bitcast_reduce_fusion.3
  292.8 0.8 fusion.105
  293.7 2.0 fusion.107
  295.7 1.8 bitcast_reduce_fusion.3
  297.5 0.8 fusion.105
  298.4 2.0 fusion.107
  300.4 1.8 bitcast_reduce_fusion.3
  302.2 0.8 fusion.105
  303.1 2.0 fusion.107
  305.1 0.3 fusion.52
  305.4 0.7 reshape.279
  306.1 0.0 all-gather.8.cloned.1.call-update
  306.1 0.0 reduce-scatter.2.cloned.1.call-start
  306.1 123.1 %all-gather.8.cloned.1.call-done = bf16[2,1024,2048]{2,1,0:T(8,128)(2,1)} async-done(((bf16[2,16,2048]{2,1,0:T(8,128)(2,1)}), bf16[2,1024,2048]{2,1,0:T(8,128)(2,1)}) %all-gather.8.cloned.1.call-update) | async-done | bytes 8388624 | tf_op jit(solution)/shard_map/all_gather | solution.py:132
  429.2 6.8 %convolution_convert_fusion = bf16[2,1024,256]{2,1,0:T(8,128)(2,1)} fusion(bf16[2,1024,2048]{2,1,0:T(8,128)(2,1)} %all-gather.8.cloned.1.call-done, bf16[2048,256]{1,0:T(8,128)(2,1)S(1)} %copy-done), kind=kOutput, calls=%fused_computation.39 | convolution fusion | flops 2148007936 | bytes 10485760 | tf_op jit(solution)/shard_map/tbf,fd->tbd/dot_general | solution.py:130
  436.0 0.0 reduce-scatter.2.cloned.1.call-update
  436.1 89.4 %reduce-scatter.2.cloned.1.call-done = bf16[2,128,256]{2,1,0:T(8,128)(2,1)} async-done(((bf16[2,1024,256]{2,1,0:T(8,128)(2,1)}), bf16[2,128,256]{2,1,0:T(8,128)(2,1)}) %reduce-scatter.2.cloned.1.call-update) | async-done | bytes 131088 | tf_op jit(solution)/shard_map/reduce_scatter | solution.py:136
  (30 shorter events, 0.4 us)
Async XLA Ops:
  6.5 422.7 %copy-start = (bf16[2048,256]{1,0:T(8,128)(2,1)S(1)}, bf16[2048,256]{1,0:T(8,128)(2,1)}, u32[]{:S(2)}) copy-start(bf16[2048,256]{1,0:T(8,128)(2,1)} %param.19) | copy-start | bytes 3145732
  6.5 139.3 %all-gather.4.cloned.1.call-start = ((), (), s32[]{:S(2)}) async-start(), calls=%async_computation.3 | async-start | bytes 4259840 | tf_op jit(solution)/shard_map/all_gather | solution.py:111
  26.7 240.0 %all-gather.6.cloned.1.call-start = ((), (), s32[]{:S(2)}) async-start(), calls=%async_computation.4 | async-start | bytes 4259840 | tf_op jit(solution)/shard_map/all_gather | solution.py:112
  39.8 389.4 %all-gather.8.cloned.1.call-start = ((), (), s32[]{:S(2)}) async-start(), calls=%async_computation.5 | async-start | bytes 8519680 | tf_op jit(solution)/shard_map/all_gather | solution.py:132
  151.2 2.0 copy-start.1
  266.8 3.6 copy-start.2
  306.1 219.4 %reduce-scatter.2.cloned.1.call-start = ((), (), s32[]{:S(2)}) async-start(), calls=%async_computation.6 | async-start | bytes 1179648 | tf_op jit(solution)/shard_map/reduce_scatter | solution.py:136
Sparse Core Ops, SparseCore 0:
  26.8 118.9 all-gather.3
  148.0 118.7 all-gather.5
  306.2 122.9 all-gather.7
  436.2 89.2 reduce-scatter.1
where the time goes:
time: 533 us; the launch traced here: 532 us
  waiting for transfers between devices  421 us (79%)
  matrix products  42.4 us (8%)
  blocking collectives  31.4 us (6%)
  local copies, waits for them, and re-layouts  14.9 us (3%)
  between operations  13.2 us (2%)
  other arithmetic  8.7 us (2%)
    all_gather x1, waiting for transfers between devices, per_device(): lax.all_gather(attended, 'seq', axis=1, tiled=True)  123 us
    all_gather x1, waiting for transfers between devices, per_device(): lax.all_gather(group_values, 'seq', axis=0, tiled=True)  113 us
    all_gather x1, waiting for transfers between devices, per_device(): lax.all_gather(group_keys, 'seq', axis=0, tiled=True)  95.6 us
    reduce_scatter x1, waiting for transfers between devices, per_device(): lax.psum_scatter(terms.astype(jnp.bfloat16), 'head', scatter_dimension=1,...  89.4 us
    all_to_all x1, blocking collectives, per_device(): lax.all_to_all(prefix_keys, 'head', split_axis=1, concat_axis=0, tiled=True)  19.2 us
    dot_general x8, matrix products, block_partial(): jnp.einsum('tbkgn,nkd->tbkgd', weights.astype(jnp.bfloat16), values_split...  17 us
    dot_general x8, matrix products, block_partial(): jnp.einsum('tbkgd,nkd->tbkgn', grouped, keys_split, preferred_element_typ...  14.6 us
    all_to_all x1, blocking collectives, per_device(): lax.all_to_all(prefix_values, 'head', split_axis=1, concat_axis=0, tiled=...  12.2 us
  transfers between devices with their start and end apart: 4, of which 4 were waited for; matrix products, arithmetic and copies ran while one was open for 3% of the time, Pallas kernels for 0%

commit v1 on v0

v1 whole, which is shorter than its diff:
```python
import functools
import math

import jax
import jax.numpy as jnp
from jax import lax
from jax.experimental import pallas as pl
from jax.experimental.pallas import tpu as pltpu
from jax.sharding import Mesh
from jax.sharding import PartitionSpec as P

HD = 128
SUF = 2
HEADS = 16
LOG2_SCALE = HD ** -0.5 * math.log2(math.e)
Y = ("u", "v")
HEAD = ("x", "w")
SEQ = ("z", "u", "v", "c")
VMEM_BYTES = 48 * 1024 * 1024


def shift(size, step):
    return [(index, (index + step) % size) for index in range(size)]


def attention_kernel(q_ref, own_ref, other_ref, out_ref):
    rows = q_ref.shape[0]
    sources = own_ref.shape[0]
    half = own_ref.shape[1] // 2
    keys = []
    values = []
    for ref in (own_ref, other_ref):
        for part in range(2):
            span = slice(part * sources // 2, (part + 1) * sources // 2)
            keys.append(ref[span, :half, :].reshape(-1, HD))
            block = ref[span, half:, :].reshape(-1, HD)
            values.append(jnp.concatenate([block, jnp.ones_like(block)], axis=1))
    lane = lax.broadcasted_iota(jnp.int32, (rows, HD), 1)
    pieces = jnp.zeros((rows, HD), jnp.float32)
    per_tile = HEADS // 2
    for tile in range(2):
        q = jnp.concatenate(
            [q_ref[:, (tile * per_tile + g) * HD : (tile * per_tile + g + 1) * HD] for g in range(per_tile)],
            axis=0,
        )
        scores = [
            lax.dot_general(q, k, (((1,), (1,)), ((), ())), preferred_element_type=jnp.float32)
            for k in keys
        ]
        top = scores[0].max(axis=1, keepdims=True)
        for s in scores[1:]:
            top = jnp.maximum(top, s.max(axis=1, keepdims=True))
        acc = None
        for s, v in zip(scores, values):
            p = jnp.exp2((s - top) * LOG2_SCALE).astype(jnp.bfloat16)
            term = jnp.dot(p, v, preferred_element_type=jnp.float32)
            acc = term if acc is None else acc + term
        total = acc[:, HD : HD + 1]
        mean = acc[:, :HD] / total
        level = top * LOG2_SCALE + jnp.log2(total)
        first = level.astype(jnp.bfloat16).astype(jnp.float32)
        rest = level - first
        second = rest.astype(jnp.bfloat16).astype(jnp.float32)
        third = rest - second
        for g in range(per_tile):
            head = tile * per_tile + g
            span = slice(g * rows, (g + 1) * rows)
            out_ref[:, head * HD : (head + 1) * HD] = mean[span].astype(jnp.bfloat16)
            for place, piece in enumerate((first, second, third)):
                pieces = jnp.where(lane == place * HEADS + head, piece[span], pieces)
    out_ref[:, HEADS * HD :] = pieces.astype(jnp.bfloat16)


def attend(q, own, other):
    rows = q.shape[0]
    return pl.pallas_call(
        attention_kernel,
        out_shape=jax.ShapeDtypeStruct((rows, HEADS * HD + HD), jnp.bfloat16),
        compiler_params=pltpu.CompilerParams(vmem_limit_bytes=VMEM_BYTES),
        name="attend",
    )(q, own, other)


def combine_kernel(q_ref, k_ref, v_ref, len_ref, m0_ref, m1_ref, m2_ref, m3_ref, out_ref):
    rows = q_ref.shape[0]
    local = rows // 2
    width = HEADS * HD
    parts = (m0_ref, m1_ref, m2_ref, m3_ref)
    lane = lax.broadcasted_iota(jnp.int32, (rows, HD), 1)
    step_one = lax.broadcasted_iota(jnp.int32, (rows, 1), 0) >= local
    used = jnp.concatenate([len_ref[...], len_ref[...]], axis=0)
    valid = (used > 0, used > 1, used >= 0, step_one)
    suffix_values = []
    logits = []
    for j in range(4):
        key = jnp.concatenate([k_ref[j], k_ref[j]], axis=0)
        suffix_values.append(jnp.concatenate([v_ref[j], v_ref[j]], axis=0))
        row = jnp.full((rows, HD), -1e30, jnp.float32)
        for g in range(HEADS):
            q = q_ref[:, g * HD : (g + 1) * HD].astype(jnp.float32)
            dot = jnp.sum(q * key, axis=1, keepdims=True) * LOG2_SCALE
            row = jnp.where(lane == g, dot, row)
        logits.append(jnp.where(valid[j], row, jnp.float32(-1e30)))
    levels = []
    for ref in parts:
        tail = ref[:, width:].astype(jnp.float32)
        level = tail + pltpu.roll(tail, HD - HEADS, 1) + pltpu.roll(tail, HD - 2 * HEADS, 1)
        levels.append(level)
    top = functools.reduce(jnp.maximum, levels + logits)
    factors = [jnp.exp2(level - top) for level in levels]
    weights = [
        jnp.where(valid[j], jnp.exp2(logits[j] - top), jnp.float32(0.0)) for j in range(4)
    ]
    total = functools.reduce(jnp.add, factors + weights)
    scale = 1.0 / total
    factors = [f * scale for f in factors]
    weights = [w * scale for w in weights]
    for g in range(HEADS):
        cols = slice(g * HD, (g + 1) * HD)
        acc = jnp.zeros((rows, HD), jnp.float32)
        for ref, f in zip(parts, factors):
            acc = acc + f[:, g : g + 1] * ref[:, cols].astype(jnp.float32)
        for j in range(4):
            acc = acc + weights[j][:, g : g + 1] * suffix_values[j]
        out_ref[:, cols] = acc.astype(jnp.bfloat16)


def combine(q, keys, values, lens, parts):
    return pl.pallas_call(
        combine_kernel,
        out_shape=jax.ShapeDtypeStruct(q.shape, jnp.bfloat16),
        compiler_params=pltpu.CompilerParams(vmem_limit_bytes=VMEM_BYTES),
        name="combine",
    )(q, keys, values, lens, *parts)


def project_kernel(place_ref, *refs):
    blocks = refs[:8]
    own_ref, other_ref, out_ref, held = refs[8:]
    rows = blocks[0].shape[0]

    @pl.when(pl.program_id(0) == 0)
    def _():
        for index, block in enumerate(blocks):
            held[index * rows : (index + 1) * rows, :] = block[...]

    first = place_ref[0]
    core = place_ref[1]
    for ref, side in ((own_ref, core), (other_ref, 1 - core)):
        terms = jnp.dot(held[...], ref[0], preferred_element_type=jnp.float32).astype(jnp.bfloat16)
        for index in range(8):
            where = lax.rem(first + index, 8)
            out_ref[0, side, where] = terms[index * rows : (index + 1) * rows]


def project(place, blocks, own, other):
    rows, depth = blocks[0].shape
    quarters, _, cols = own.shape
    whole = pl.BlockSpec((rows, depth), lambda i, place: (0, 0))
    part = pl.BlockSpec((1, depth, cols), lambda i, place: (i, 0, 0))
    return pl.pallas_call(
        project_kernel,
        out_shape=jax.ShapeDtypeStruct((quarters, 2, 8, rows, cols), jnp.bfloat16),
        grid_spec=pltpu.PrefetchScalarGridSpec(
            num_scalar_prefetch=1,
            grid=(quarters,),
            in_specs=[whole] * 8 + [part, part],
            out_specs=pl.BlockSpec((1, 2, 8, rows, cols), lambda i, place: (i, 0, 0, 0, 0)),
            scratch_shapes=[pltpu.VMEM((8 * rows, depth), jnp.bfloat16)],
        ),
        compiler_params=pltpu.CompilerParams(vmem_limit_bytes=VMEM_BYTES),
        name="project",
    )(place, *blocks, own, other)


def per_device(
    queries,
    prefix_keys,
    prefix_values,
    cache_keys,
    cache_values,
    new_keys,
    new_values,
    suffix_len,
    out_weight,
):
    local = queries.shape[1]
    count = prefix_keys.shape[0]
    q = queries.reshape(2 * local, HEADS * HD)

    weight_y = lax.all_gather(out_weight, Y, axis=0, tiled=False)

    q_parts = [q] + [lax.ppermute(q, Y, shift(4, k)) for k in (1, 2, 3)]

    split = [
        jnp.swapaxes(rows.reshape(count, 8, HD), 0, 1) for rows in (prefix_keys, prefix_values)
    ]
    sent = jnp.concatenate(split, axis=1)
    sent = jnp.broadcast_to(sent[None], (8,) + sent.shape).reshape(64, 2 * count, HD)
    own = lax.all_to_all(sent, ("z",) + HEAD, 0, 0, tiled=True)
    other = lax.ppermute(own, "c", shift(2, 1))

    parts = [None] * 4
    for k in (2, 1, 3, 0):
        message = attend(q_parts[k], own, other)
        parts[k] = message if k == 0 else lax.ppermute(message, Y, shift(4, -k))

    suffix_keys = jnp.stack(
        [cache_keys[:, 0], cache_keys[:, 1], new_keys[0], new_keys[1]], axis=0
    ).astype(jnp.float32)
    suffix_values = jnp.stack(
        [cache_values[:, 0], cache_values[:, 1], new_values[0], new_values[1]], axis=0
    ).astype(jnp.float32)
    attended = combine(q, suffix_keys, suffix_values, suffix_len.reshape(local, 1), parts)

    blocks = {0: attended}
    up = attended
    down = attended
    for step in range(1, 5):
        up = lax.ppermute(up, "z", shift(8, 1))
        blocks[-step] = up
        if step < 4:
            down = lax.ppermute(down, "z", shift(8, -1))
            blocks[step] = down
    weight_other = lax.ppermute(weight_y, "c", shift(2, 1))
    place = jnp.stack([lax.rem(lax.axis_index("z") + 4, 8), lax.axis_index("c")]).astype(jnp.int32)
    terms = project(place, [blocks[offset] for offset in range(-4, 4)], weight_y, weight_other)

    rows, cols = terms.shape[3:]
    arrived = lax.all_to_all(
        terms.reshape(64, rows, cols), Y + ("c",) + HEAD, 0, 0, tiled=True
    ).reshape(8, 8, 2, local, cols)
    summed = jnp.sum(arrived.astype(jnp.float32), axis=1).astype(jnp.bfloat16)
    return jnp.swapaxes(summed, 0, 1).reshape(2, 8 * local, cols)


def solution(mesh):
    split_mesh = Mesh(mesh.devices.reshape(8, 2, 2, 2, 4, 2), SEQ + HEAD)
    in_specs = (
        P(None, SEQ, HEAD),
        P(SEQ + HEAD, None),
        P(SEQ + HEAD, None),
        P(SEQ, None, HEAD),
        P(SEQ, None, HEAD),
        P(None, SEQ, HEAD),
        P(None, SEQ, HEAD),
        P(SEQ),
        P(HEAD, SEQ),
    )
    out_specs = P(None, HEAD, SEQ)
    return jax.shard_map(
        per_device, mesh=split_mesh, in_specs=in_specs, out_specs=out_specs, check_vma=False
    )
```

time: 533 us -> 286 us (0.54)
  the two profiles are of different devices: /device:TPU:1 before, /device:TPU:9 now
where the time goes in v1:
time: 286 us; the launch traced here: 285 us
  waiting for transfers between devices  107 us (37%)
  blocking collectives  85.5 us (30%)
  starting transfers between devices  50.5 us (18%)
  Pallas kernels  25.7 us (9%)
  between operations  13.8 us (5%)
    all_gather x1, waiting for transfers between devices, per_device(): weight_y = lax.all_gather(out_weight, Y, axis=0, tiled=False)  93.5 us
    all_to_all x1, blocking collectives, per_device(): lax.all_to_all(terms.reshape(64, rows, cols), Y + ('c',) + HEAD, 0, 0, ti...  43.7 us
    all_to_all x1, blocking collectives, per_device(): own = lax.all_to_all(sent, ('z',) + HEAD, 0, 0, tiled=True)  41.7 us
    pallas_call x4, Pallas kernels, attend(): pl.pallas_call(attention_kernel, out_shape=jax.ShapeDtypeStruct((rows, HE...  18.6 us
    ppermute x3, starting transfers between devices, per_device(): q_parts = [q] + [lax.ppermute(q, Y, shift(4, k)) for k in (1, 2, 3)]  13.8 us
    ppermute x3, starting transfers between devices, per_device(): down = lax.ppermute(down, 'z', shift(8, -1))  13.5 us
    ppermute x3, starting transfers between devices, per_device(): parts[k] = message if k == 0 else lax.ppermute(message, Y, shift(4, -k))  9.3 us
    ppermute x4, starting transfers between devices, per_device(): up = lax.ppermute(up, 'z', shift(8, 1))  7.83 us
  transfers between devices with their start and end apart: 16, of which 6 were waited for; matrix products, arithmetic and copies ran while one was open for 1% of the time, Pallas kernels for 7%

profile of v1, /device:TPU:9, one launch (start us, length us, event | category | flops | bytes accessed | tf_op | source)
XLA Modules:
  0.0 285.1 jit_solution(12556792969256324961)
XLA Ops:
  6.5 0.0 copy-start
  6.5 0.0 copy-start.1
  6.5 0.0 copy-start.2
  6.5 0.0 all-gather.3.cloned.1.call-start
  6.5 0.7 all-gather.3.cloned.1.call-update
  7.3 93.5 %all-gather.3.cloned.1.call-done = bf16[8192,256]{1,0:T(8,128)(2,1)} async-done(((bf16[2048,256]{1,0:T(8,128)(2,1)}), bf16[8192,256]{1,0:T(8,128)(2,1)}) %all-gather.3.cloned.1.call-update) | async-done | bytes 4194320 | tf_op jit(solution)/shard_map/all_gather | solution.py:191
  100.8 2.6 collective-permute-start.14
  103.3 0.9 copy.33
  104.2 0.9 copy.34
  105.1 0.2 broadcast_in_dim.2
  105.3 0.0 copy-start.3
  105.4 0.0 copy-start.5
  105.4 0.0 copy-start.4
  105.4 41.7 %all_to_all.10.own_ref = bf16[64,64,128]{2,1,0:T(8,128)(2,1)S(1)} all-to-all(bf16[64,64,128]{2,1,0:T(8,128)(2,1)S(1)} %bitcast.35), channel_id=1, replica_groups=mesh['z'=8,'u'=2,'v'=2,'c'=2,'x'=4,'w'=2] {'z','x','w'}, dimensions={0} | all-to-all | bytes 2097152 | tf_op jit(solution)/shard_map/all_to_all | solution.py:200
  147.1 3.5 %collective-permute-start = (bf16[64,64,128]{2,1,0:T(8,128)(2,1)S(1)}, bf16[64,64,128]{2,1,0:T(8,128)(2,1)S(1)}, u32[]{:S(2)}, u32[]{:S(2)}) collective-permute-start(bf16[64,64,128]{2,1,0:T(8,128)(2,1)S(1)} %all_to_all.10.own_ref), channel_id=1, source_target_pairs={{0,8},{8,0},{1,9},{9,1},{2,10},{10,2},{3,11},{11,3},{4,12},{12,4},... | collective-permute-start | bytes 3145736 | tf_op jit(solution)/shard_map/ppermute | solution.py:201
  150.6 0.0 copy-done
  150.6 2.5 collective-permute-start.5
  153.1 8.5 %collective-permute-start.3 = (bf16[32,2048]{1,0:T(8,128)(2,1)S(1)}, bf16[32,2048]{1,0:T(8,128)(2,1)S(1)}, u32[]{:S(2)}, u32[]{:S(2)}) collective-permute-start(bf16[32,2048]{1,0:T(8,128)(2,1)S(1)} %bitcast.28), channel_id=1, source_target_pairs={{0,32},{16,48},{32,0},{48,16},{1,33},{17,49},{33,1},{49,17},{2,34}... | collective-permute-start | bytes 393224 | tf_op jit(solution)/shard_map/ppermute | solution.py:193
  161.6 2.8 collective-permute-start.1
  164.4 0.0 copy-done.1
  164.4 0.0 copy-done.2
  164.5 6.3 %collective-permute-done.1.q_ref = bf16[32,2048]{1,0:T(8,128)(2,1)S(1)} collective-permute-done((bf16[32,2048]{1,0:T(8,128)(2,1)S(1)}, bf16[32,2048]{1,0:T(8,128)(2,1)S(1)}, u32[]{:S(2)}, u32[]{:S(2)}) %collective-permute-start.1) | collective-permute-done | bytes 131104 | tf_op jit(solution)/shard_map/ppermute | solution.py:193
  170.8 0.0 collective-permute-done.other_ref
  170.8 4.6 %attend.5 = bf16[32,2176]{1,0:T(8,128)(2,1)S(1)} custom-call(bf16[32,2048]{1,0:T(8,128)(2,1)S(1)} %collective-permute-done.1.q_ref, bf16[64,64,128]{2,1,0:T(8,128)(2,1)S(1)} %all_to_all.10.own_ref, bf16[64,64,128]{2,1,0:T(8,128)(2,1)S(1)} %collective-permute-done.other_ref), custom_call_target="tpu_custom_call" | custom-call | tf_op jit(solution)/shard_map/attend/pallas_call | solution.py:76
  175.4 1.9 collective-permute-start.2
  177.4 0.0 collective-permute-done.3.q_ref
  177.4 4.6 %attend.6 = bf16[32,2176]{1,0:T(8,128)(2,1)S(1)} custom-call(bf16[32,2048]{1,0:T(8,128)(2,1)S(1)} %collective-permute-done.3.q_ref, bf16[64,64,128]{2,1,0:T(8,128)(2,1)S(1)} %all_to_all.10.own_ref, bf16[64,64,128]{2,1,0:T(8,128)(2,1)S(1)} %collective-permute-done.other_ref), custom_call_target="tpu_custom_call" | custom-call | tf_op jit(solution)/shard_map/attend/pallas_call | solution.py:76
  182.0 5.5 %collective-permute-start.4 = (bf16[32,2176]{1,0:T(8,128)(2,1)S(1)}, bf16[32,2176]{1,0:T(8,128)(2,1)S(1)}, u32[]{:S(2)}, u32[]{:S(2)}) collective-permute-start(bf16[32,2176]{1,0:T(8,128)(2,1)S(1)} %attend.6), channel_id=1, source_target_pairs={{0,32},{16,48},{32,0},{48,16},{1,33},{17,49},{33,1},{49,17},{2,34}... | collective-permute-start | bytes 417800 | tf_op jit(solution)/shard_map/ppermute | solution.py:206
  187.5 0.0 collective-permute-done.5.q_ref
  187.5 4.6 %attend.7 = bf16[32,2176]{1,0:T(8,128)(2,1)S(1)} custom-call(bf16[32,2048]{1,0:T(8,128)(2,1)S(1)} %collective-permute-done.5.q_ref, bf16[64,64,128]{2,1,0:T(8,128)(2,1)S(1)} %all_to_all.10.own_ref, bf16[64,64,128]{2,1,0:T(8,128)(2,1)S(1)} %collective-permute-done.other_ref), custom_call_target="tpu_custom_call" | custom-call | tf_op jit(solution)/shard_map/attend/pallas_call | solution.py:76
  192.2 1.9 collective-permute-start.6
  194.1 0.0 copy-done.3
  194.1 0.0 copy-done.5
  194.1 0.1 copy.27.len_ref
  194.2 0.0 copy-done.4
  194.2 4.6 %attend.4.m0_ref = bf16[32,2176]{1,0:T(8,128)(2,1)S(1)} custom-call(bf16[32,2048]{1,0:T(8,128)(2,1)S(1)} %bitcast.30, bf16[64,64,128]{2,1,0:T(8,128)(2,1)S(1)} %all_to_all.10.own_ref, bf16[64,64,128]{2,1,0:T(8,128)(2,1)S(1)} %collective-permute-done.other_ref), custom_call_target="tpu_custom_call" | custom-call | tf_op jit(solution)/shard_map/attend/pallas_call | solution.py:76
  198.9 0.0 collective-permute-done.2.m1_ref
  198.9 0.0 collective-permute-done.4.m2_ref
  198.9 0.0 collective-permute-done.6.m3_ref
  198.9 1.0 combine.1.refs_4_
  200.0 2.1 collective-permute-start.7
  202.1 4.4 %collective-permute-start.11 = (bf16[32,2048]{1,0:T(8,128)(2,1)S(1)}, bf16[32,2048]{1,0:T(8,128)(2,1)S(1)}, u32[]{:S(2)}, u32[]{:S(2)}) collective-permute-start(bf16[32,2048]{1,0:T(8,128)(2,1)S(1)} %combine.1.refs_4_), channel_id=1, source_target_pairs={{0,448},{64,0},{128,64},{192,128},{256,192},{320,256},{384,320},{4... | collective-permute-start | bytes 393224 | tf_op jit(solution)/shard_map/ppermute | solution.py:223
  206.5 0.4 collective-permute-done.7.refs_3_
  206.9 1.9 collective-permute-start.8
  208.8 0.0 collective-permute-done.11.refs_5_
  208.8 4.6 %collective-permute-start.12 = (bf16[32,2048]{1,0:T(8,128)(2,1)S(1)}, bf16[32,2048]{1,0:T(8,128)(2,1)S(1)}, u32[]{:S(2)}, u32[]{:S(2)}) collective-permute-start(bf16[32,2048]{1,0:T(8,128)(2,1)S(1)} %collective-permute-done.11.refs_5_), channel_id=1, source_target_pairs={{0,448},{64,0},{128,64},{192,128},{256,192},{320,256},{384,320},{4... | collective-permute-start | bytes 393224 | tf_op jit(solution)/shard_map/ppermute | solution.py:223
  213.4 0.4 collective-permute-done.8.refs_2_
  213.8 1.9 collective-permute-start.9
  215.7 0.0 collective-permute-done.12.refs_6_
  215.7 4.6 %collective-permute-start.13 = (bf16[32,2048]{1,0:T(8,128)(2,1)S(1)}, bf16[32,2048]{1,0:T(8,128)(2,1)S(1)}, u32[]{:S(2)}, u32[]{:S(2)}) collective-permute-start(bf16[32,2048]{1,0:T(8,128)(2,1)S(1)} %collective-permute-done.12.refs_6_), channel_id=1, source_target_pairs={{0,448},{64,0},{128,64},{192,128},{256,192},{320,256},{384,320},{4... | collective-permute-start | bytes 393224 | tf_op jit(solution)/shard_map/ppermute | solution.py:223
  220.3 0.4 collective-permute-done.9.refs_1_
  220.7 1.9 collective-permute-start.10
  222.6 0.1 pad_add_fusion.place_ref
  222.7 0.0 collective-permute-done.13.refs_7_
  222.7 4.9 %collective-permute-done.10.refs_0_ = bf16[32,2048]{1,0:T(8,128)(2,1)S(1)} collective-permute-done((bf16[32,2048]{1,0:T(8,128)(2,1)S(1)}, bf16[32,2048]{1,0:T(8,128)(2,1)S(1)}, u32[]{:S(2)}, u32[]{:S(2)}) %collective-permute-start.10) | collective-permute-done | bytes 131104 | tf_op jit(solution)/shard_map/ppermute | solution.py:220
  227.6 0.0 collective-permute-done.14.refs_9_
  227.6 6.1 %project.1 = bf16[4,2,8,32,256]{4,3,2,1,0:T(8,128)(2,1)S(1)} custom-call(s32[2]{0:T(128)S(1)} %pad_add_fusion.place_ref, bf16[32,2048]{1,0:T(8,128)(2,1)S(1)} %collective-permute-done.10.refs_0_, bf16[32,2048]{1,0:T(8,128)(2,1)S(1)} %collective-permute-done.9.refs_1_, bf16[32,2048]{1,0:T(8,128)(2,1)S(1)} %collective-permute-done.8.refs_2_, ...), custom_call_target="tpu_custom_call" | custom-call | tf_op jit(solution)/shard_map/project/pallas_call | solution.py:161
  233.7 43.7 %all_to_all.11 = bf16[64,32,256]{2,1,0:T(8,128)(2,1)S(1)} all-to-all(bf16[64,32,256]{2,1,0:T(8,128)(2,1)S(1)} %bitcast.26), channel_id=1, replica_groups=mesh['z'=8,'u'=2,'v'=2,'c'=2,'x'=4,'w'=2] {'u','v','c','x','w'}, dimensions={0} | all-to-all | bytes 2097152 | tf_op jit(solution)/shard_map/all_to_all | solution.py:230
  277.4 0.2 reduce_sum.12
  277.6 0.7 copy.28
  (8 shorter events, 0.1 us)
Async XLA Ops:
  6.5 144.0 %copy-start = (bf16[2,16,2048]{2,1,0:T(8,128)(2,1)S(1)}, bf16[2,16,2048]{2,1,0:T(8,128)(2,1)}, u32[]{:S(2)}) copy-start(bf16[2,16,2048]{2,1,0:T(8,128)(2,1)} %param.9) | copy-start | bytes 393220
  6.5 157.9 %copy-start.1 = (bf16[16,2,128]{2,1,0:T(2,128)(2,1)S(1)}, bf16[16,2,128]{2,1,0:T(2,128)(2,1)}, u32[]{:S(2)}) copy-start(bf16[16,2,128]{2,1,0:T(2,128)(2,1)} %param.12) | copy-start | bytes 24580
  6.5 157.9 %copy-start.2 = (bf16[16,2,128]{2,1,0:T(2,128)(2,1)S(1)}, bf16[16,2,128]{2,1,0:T(2,128)(2,1)}, u32[]{:S(2)}) copy-start(bf16[16,2,128]{2,1,0:T(2,128)(2,1)} %param.13) | copy-start | bytes 24580
  6.5 94.2 %all-gather.3.cloned.1.call-start = ((), (), s32[]{:S(2)}) async-start(), calls=%async_computation.2 | async-start | bytes 5242880 | tf_op jit(solution)/shard_map/all_gather | solution.py:191
  100.8 126.9 %collective-permute-start.14 = (bf16[4,2048,256]{2,1,0:T(8,128)(2,1)}, bf16[4,2048,256]{2,1,0:T(8,128)(2,1)}, u32[]{:S(2)}, u32[]{:S(2)}) collective-permute-start(bf16[4,2048,256]{2,1,0:T(8,128)(2,1)} %bitcast.32), channel_id=1, source_target_pairs={{0,8},{8,0},{1,9},{9,1},{2,10},{10,2},{3,11},{11,3},{4,12},{12,4},... | collective-permute-start | bytes 12582920 | tf_op jit(solution)/shard_map/ppermute | solution.py:225
  105.3 88.8 %copy-start.3 = (bf16[2,16,128]{2,1,0:T(8,128)(2,1)S(1)}, bf16[2,16,128]{2,1,0:T(8,128)(2,1)}, u32[]{:S(2)}) copy-start(bf16[2,16,128]{2,1,0:T(8,128)(2,1)} %param.15) | copy-start | bytes 24580
  105.4 88.8 %copy-start.5 = (s32[16]{0:T(128)S(1)}, s32[16]{0:T(128)}, u32[]{:S(2)}) copy-start(s32[16]{0:T(128)} %param.16) | copy-start | bytes 196
  105.4 88.8 %copy-start.4 = (bf16[2,16,128]{2,1,0:T(8,128)(2,1)S(1)}, bf16[2,16,128]{2,1,0:T(8,128)(2,1)}, u32[]{:S(2)}) copy-start(bf16[2,16,128]{2,1,0:T(8,128)(2,1)} %param.14) | copy-start | bytes 24580
  147.1 23.7 %collective-permute-start = (bf16[64,64,128]{2,1,0:T(8,128)(2,1)S(1)}, bf16[64,64,128]{2,1,0:T(8,128)(2,1)S(1)}, u32[]{:S(2)}, u32[]{:S(2)}) collective-permute-start(bf16[64,64,128]{2,1,0:T(8,128)(2,1)S(1)} %all_to_all.10.own_ref), channel_id=1, source_target_pairs={{0,8},{8,0},{1,9},{9,1},{2,10},{10,2},{3,11},{11,3},{4,12},{12,4},... | collective-permute-start | bytes 3145736 | tf_op jit(solution)/shard_map/ppermute | solution.py:201
  150.6 36.9 %collective-permute-start.5 = (bf16[32,2048]{1,0:T(8,128)(2,1)S(1)}, bf16[32,2048]{1,0:T(8,128)(2,1)S(1)}, u32[]{:S(2)}, u32[]{:S(2)}) collective-permute-start(bf16[32,2048]{1,0:T(8,128)(2,1)S(1)} %bitcast.27), channel_id=1, source_target_pairs={{0,48},{16,0},{32,16},{48,32},{1,49},{17,1},{33,17},{49,33},{2,50}... | collective-permute-start | bytes 393224 | tf_op jit(solution)/shard_map/ppermute | solution.py:193
  153.1 24.3 %collective-permute-start.3 = (bf16[32,2048]{1,0:T(8,128)(2,1)S(1)}, bf16[32,2048]{1,0:T(8,128)(2,1)S(1)}, u32[]{:S(2)}, u32[]{:S(2)}) collective-permute-start(bf16[32,2048]{1,0:T(8,128)(2,1)S(1)} %bitcast.28), channel_id=1, source_target_pairs={{0,32},{16,48},{32,0},{48,16},{1,33},{17,49},{33,1},{49,17},{2,34}... | collective-permute-start | bytes 393224 | tf_op jit(solution)/shard_map/ppermute | solution.py:193
  161.6 9.2 %collective-permute-start.1 = (bf16[32,2048]{1,0:T(8,128)(2,1)S(1)}, bf16[32,2048]{1,0:T(8,128)(2,1)S(1)}, u32[]{:S(2)}, u32[]{:S(2)}) collective-permute-start(bf16[32,2048]{1,0:T(8,128)(2,1)S(1)} %bitcast.29), channel_id=1, source_target_pairs={{0,16},{16,32},{32,48},{48,0},{1,17},{17,33},{33,49},{49,1},{2,18}... | collective-permute-start | bytes 393224 | tf_op jit(solution)/shard_map/ppermute | solution.py:193
  175.4 23.4 %collective-permute-start.2 = (bf16[32,2176]{1,0:T(8,128)(2,1)S(1)}, bf16[32,2176]{1,0:T(8,128)(2,1)S(1)}, u32[]{:S(2)}, u32[]{:S(2)}) collective-permute-start(bf16[32,2176]{1,0:T(8,128)(2,1)S(1)} %attend.5), channel_id=1, source_target_pairs={{0,48},{16,0},{32,16},{48,32},{1,49},{17,1},{33,17},{49,33},{2,50}... | collective-permute-start | bytes 417800 | tf_op jit(solution)/shard_map/ppermute | solution.py:206
  182.0 16.9 %collective-permute-start.4 = (bf16[32,2176]{1,0:T(8,128)(2,1)S(1)}, bf16[32,2176]{1,0:T(8,128)(2,1)S(1)}, u32[]{:S(2)}, u32[]{:S(2)}) collective-permute-start(bf16[32,2176]{1,0:T(8,128)(2,1)S(1)} %attend.6), channel_id=1, source_target_pairs={{0,32},{16,48},{32,0},{48,16},{1,33},{17,49},{33,1},{49,17},{2,34}... | collective-permute-start | bytes 417800 | tf_op jit(solution)/shard_map/ppermute | solution.py:206
  192.2 6.7 %collective-permute-start.6 = (bf16[32,2176]{1,0:T(8,128)(2,1)S(1)}, bf16[32,2176]{1,0:T(8,128)(2,1)S(1)}, u32[]{:S(2)}, u32[]{:S(2)}) collective-permute-start(bf16[32,2176]{1,0:T(8,128)(2,1)S(1)} %attend.7), channel_id=1, source_target_pairs={{0,16},{16,32},{32,48},{48,0},{1,17},{17,33},{33,49},{49,1},{2,18}... | collective-permute-start | bytes 417800 | tf_op jit(solution)/shard_map/ppermute | solution.py:206
  200.0 6.9 %collective-permute-start.7 = (bf16[32,2048]{1,0:T(8,128)(2,1)S(1)}, bf16[32,2048]{1,0:T(8,128)(2,1)S(1)}, u32[]{:S(2)}, u32[]{:S(2)}) collective-permute-start(bf16[32,2048]{1,0:T(8,128)(2,1)S(1)} %combine.1.refs_4_), channel_id=1, source_target_pairs={{0,64},{64,128},{128,192},{192,256},{256,320},{320,384},{384,448},... | collective-permute-start | bytes 393224 | tf_op jit(solution)/shard_map/ppermute | solution.py:220
  202.1 6.7 %collective-permute-start.11 = (bf16[32,2048]{1,0:T(8,128)(2,1)S(1)}, bf16[32,2048]{1,0:T(8,128)(2,1)S(1)}, u32[]{:S(2)}, u32[]{:S(2)}) collective-permute-start(bf16[32,2048]{1,0:T(8,128)(2,1)S(1)} %combine.1.refs_4_), channel_id=1, source_target_pairs={{0,448},{64,0},{128,64},{192,128},{256,192},{320,256},{384,320},{4... | collective-permute-start | bytes 393224 | tf_op jit(solution)/shard_map/ppermute | solution.py:223
  206.9 6.9 %collective-permute-start.8 = (bf16[32,2048]{1,0:T(8,128)(2,1)S(1)}, bf16[32,2048]{1,0:T(8,128)(2,1)S(1)}, u32[]{:S(2)}, u32[]{:S(2)}) collective-permute-start(bf16[32,2048]{1,0:T(8,128)(2,1)S(1)} %collective-permute-done.7.refs_3_), channel_id=1, source_target_pairs={{0,64},{64,128},{128,192},{192,256},{256,320},{320,384},{384,448},... | collective-permute-start | bytes 393224 | tf_op jit(solution)/shard_map/ppermute | solution.py:220
  208.8 6.9 %collective-permute-start.12 = (bf16[32,2048]{1,0:T(8,128)(2,1)S(1)}, bf16[32,2048]{1,0:T(8,128)(2,1)S(1)}, u32[]{:S(2)}, u32[]{:S(2)}) collective-permute-start(bf16[32,2048]{1,0:T(8,128)(2,1)S(1)} %collective-permute-done.11.refs_5_), channel_id=1, source_target_pairs={{0,448},{64,0},{128,64},{192,128},{256,192},{320,256},{384,320},{4... | collective-permute-start | bytes 393224 | tf_op jit(solution)/shard_map/ppermute | solution.py:223
  213.8 6.9 %collective-permute-start.9 = (bf16[32,2048]{1,0:T(8,128)(2,1)S(1)}, bf16[32,2048]{1,0:T(8,128)(2,1)S(1)}, u32[]{:S(2)}, u32[]{:S(2)}) collective-permute-start(bf16[32,2048]{1,0:T(8,128)(2,1)S(1)} %collective-permute-done.8.refs_2_), channel_id=1, source_target_pairs={{0,64},{64,128},{128,192},{192,256},{256,320},{320,384},{384,448},... | collective-permute-start | bytes 393224 | tf_op jit(solution)/shard_map/ppermute | solution.py:220
  215.7 7.0 %collective-permute-start.13 = (bf16[32,2048]{1,0:T(8,128)(2,1)S(1)}, bf16[32,2048]{1,0:T(8,128)(2,1)S(1)}, u32[]{:S(2)}, u32[]{:S(2)}) collective-permute-start(bf16[32,2048]{1,0:T(8,128)(2,1)S(1)} %collective-permute-done.12.refs_6_), channel_id=1, source_target_pairs={{0,448},{64,0},{128,64},{192,128},{256,192},{320,256},{384,320},{4... | collective-permute-start | bytes 393224 | tf_op jit(solution)/shard_map/ppermute | solution.py:223
  220.7 6.9 %collective-permute-start.10 = (bf16[32,2048]{1,0:T(8,128)(2,1)S(1)}, bf16[32,2048]{1,0:T(8,128)(2,1)S(1)}, u32[]{:S(2)}, u32[]{:S(2)}) collective-permute-start(bf16[32,2048]{1,0:T(8,128)(2,1)S(1)} %collective-permute-done.9.refs_1_), channel_id=1, source_target_pairs={{0,64},{64,128},{128,192},{192,256},{256,320},{320,384},{384,448},... | collective-permute-start | bytes 393224 | tf_op jit(solution)/shard_map/ppermute | solution.py:220
Sparse Core Ops, SparseCore 0:
  9.5 91.2 all-gather.2

commit v2 on v1

v2 whole, which is shorter than its diff:
```python
import functools
import math

import jax
import jax.numpy as jnp
from jax import lax
from jax.experimental import pallas as pl
from jax.experimental.pallas import tpu as pltpu
from jax.sharding import Mesh
from jax.sharding import PartitionSpec as P

HD = 128
SUF = 2
HEADS = 16
LOG2_SCALE = HD ** -0.5 * math.log2(math.e)
Y = ("u", "v")
HEAD = ("x", "w")
SEQ = ("z", "u", "v", "c")
CHUNK = 8
EARLY = 1280
VMEM_BYTES = 48 * 1024 * 1024


def shift(size, step):
    return [(index, (index + step) % size) for index in range(size)]


def partner(size, bits):
    return [(index, index ^ bits) for index in range(size)]


def ring(value):
    blocks = {0: value}
    up = value
    down = value
    for step in range(1, 5):
        up = lax.ppermute(up, "z", shift(8, 1))
        blocks[-step] = up
        if step < 4:
            down = lax.ppermute(down, "z", shift(8, -1))
            blocks[step] = down
        yield blocks


def swap(value):
    return lax.ppermute(value, "c", partner(2, 1))


def after(value, *others, space=pl.ANY):
    def nothing(*refs):
        pass

    return pl.pallas_call(
        nothing,
        out_shape=jax.ShapeDtypeStruct(value.shape, value.dtype),
        in_specs=[pl.BlockSpec(memory_space=space)] + [pl.BlockSpec(memory_space=pl.ANY)] * len(others),
        out_specs=pl.BlockSpec(memory_space=space),
        input_output_aliases={0: 0},
        name="after",
    )(value, *others)


def attention_kernel(q_ref, *refs):
    out_ref = refs[-1]
    rows = q_ref.shape[0]
    half = refs[0].shape[1] // 2
    q = jnp.concatenate([q_ref[:, g * HD : (g + 1) * HD] for g in range(HEADS)], axis=0)
    top = None
    acc = None
    for ref in refs[:-1]:
        for start in range(0, ref.shape[0], CHUNK):
            span = slice(start, start + CHUNK)
            keys = ref[span, :half, :].reshape(-1, HD)
            block = ref[span, half:, :].reshape(-1, HD)
            values = jnp.concatenate([block, jnp.ones_like(block)], axis=1)
            scores = lax.dot_general(
                q, keys, (((1,), (1,)), ((), ())), preferred_element_type=jnp.float32
            )
            highest = scores.max(axis=1, keepdims=True)
            if top is not None:
                highest = jnp.maximum(top, highest)
            weights = jnp.exp2((scores - highest) * LOG2_SCALE).astype(jnp.bfloat16)
            term = jnp.dot(weights, values, preferred_element_type=jnp.float32)
            acc = term if acc is None else acc * jnp.exp2((top - highest) * LOG2_SCALE) + term
            top = highest
    total = acc[:, HD : HD + 1]
    mean = acc[:, :HD] / total
    level = top * LOG2_SCALE + jnp.log2(total)
    first = level.astype(jnp.bfloat16).astype(jnp.float32)
    rest = level - first
    second = rest.astype(jnp.bfloat16).astype(jnp.float32)
    third = rest - second
    lane = lax.broadcasted_iota(jnp.int32, (rows, HD), 1)
    pieces = jnp.zeros((rows, HD), jnp.float32)
    for g in range(HEADS):
        span = slice(g * rows, (g + 1) * rows)
        out_ref[:, g * HD : (g + 1) * HD] = mean[span].astype(jnp.bfloat16)
        for place, piece in enumerate((first, second, third)):
            pieces = jnp.where(lane == place * HEADS + g, piece[span], pieces)
    out_ref[:, HEADS * HD :] = pieces.astype(jnp.bfloat16)


def attend(q, blocks):
    rows = q.shape[0]
    return pl.pallas_call(
        attention_kernel,
        out_shape=jax.ShapeDtypeStruct((rows, HEADS * HD + HD), jnp.bfloat16),
        compiler_params=pltpu.CompilerParams(vmem_limit_bytes=VMEM_BYTES),
        name="attend",
    )(q, *blocks)


def combine_kernel(q_ref, k_ref, v_ref, len_ref, m0_ref, m1_ref, m2_ref, m3_ref, out_ref):
    rows = q_ref.shape[0]
    local = rows // 2
    width = HEADS * HD
    parts = (m0_ref, m1_ref, m2_ref, m3_ref)
    lane = lax.broadcasted_iota(jnp.int32, (rows, HD), 1)
    step_one = lax.broadcasted_iota(jnp.int32, (rows, 1), 0) >= local
    used = jnp.concatenate([len_ref[...], len_ref[...]], axis=0)
    valid = (used > 0, used > 1, used >= 0, step_one)
    suffix_values = []
    logits = []
    for j in range(4):
        key = jnp.concatenate([k_ref[j], k_ref[j]], axis=0)
        suffix_values.append(jnp.concatenate([v_ref[j], v_ref[j]], axis=0))
        row = jnp.full((rows, HD), -1e30, jnp.float32)
        for g in range(HEADS):
            q = q_ref[:, g * HD : (g + 1) * HD].astype(jnp.float32)
            dot = jnp.sum(q * key, axis=1, keepdims=True) * LOG2_SCALE
            row = jnp.where(lane == g, dot, row)
        logits.append(jnp.where(valid[j], row, jnp.float32(-1e30)))
    levels = []
    for ref in parts:
        tail = ref[:, width:].astype(jnp.float32)
        level = tail + pltpu.roll(tail, HD - HEADS, 1) + pltpu.roll(tail, HD - 2 * HEADS, 1)
        levels.append(level)
    top = functools.reduce(jnp.maximum, levels + logits)
    factors = [jnp.exp2(level - top) for level in levels]
    weights = [
        jnp.where(valid[j], jnp.exp2(logits[j] - top), jnp.float32(0.0)) for j in range(4)
    ]
    total = functools.reduce(jnp.add, factors + weights)
    scale = 1.0 / total
    factors = [f * scale for f in factors]
    weights = [w * scale for w in weights]
    for g in range(HEADS):
        cols = slice(g * HD, (g + 1) * HD)
        acc = jnp.zeros((rows, HD), jnp.float32)
        for ref, f in zip(parts, factors):
            acc = acc + f[:, g : g + 1] * ref[:, cols].astype(jnp.float32)
        for j in range(4):
            acc = acc + weights[j][:, g : g + 1] * suffix_values[j]
        out_ref[:, cols] = acc.astype(jnp.bfloat16)


def combine(q, keys, values, lens, parts):
    return pl.pallas_call(
        combine_kernel,
        out_shape=jax.ShapeDtypeStruct(q.shape, jnp.bfloat16),
        compiler_params=pltpu.CompilerParams(vmem_limit_bytes=VMEM_BYTES),
        name="combine",
    )(q, keys, values, lens, *parts)


def project_kernel(place_ref, *refs):
    blocks = refs[:-4]
    early_ref, late_ref, out_ref, held = refs[-4:]
    rows = out_ref.shape[3]

    @pl.when(pl.program_id(0) == 0)
    def _():
        start = 0
        for block in blocks:
            held[start : start + block.shape[0], :] = block[...]
            start += block.shape[0]

    first = place_ref[0]
    core = place_ref[1]
    depth = early_ref.shape[1]
    terms = jnp.dot(held[:, :depth], early_ref[0], preferred_element_type=jnp.float32)
    terms += jnp.dot(held[:, depth:], late_ref[0], preferred_element_type=jnp.float32)
    terms = terms.astype(jnp.bfloat16)
    for side in range(2):
        which = core if side == 0 else 1 - core
        for index in range(8):
            where = lax.rem(first + index, 8)
            start = (side * 8 + index) * rows
            out_ref[0, where, which] = terms[start : start + rows]


def project(place, blocks, weights):
    depth = blocks[0].shape[1]
    quarters, _, cols = weights[0].shape
    rows = sum(block.shape[0] for block in blocks) // 16
    whole = [pl.BlockSpec(block.shape, lambda i, place: (0, 0)) for block in blocks]
    return pl.pallas_call(
        project_kernel,
        out_shape=jax.ShapeDtypeStruct((quarters, 8, 2, rows, cols), jnp.bfloat16),
        grid_spec=pltpu.PrefetchScalarGridSpec(
            num_scalar_prefetch=1,
            grid=(quarters,),
            in_specs=whole
            + [pl.BlockSpec((1,) + part.shape[1:], lambda i, place: (i, 0, 0)) for part in weights],
            out_specs=pl.BlockSpec((1, 8, 2, rows, cols), lambda i, place: (i, 0, 0, 0, 0)),
            scratch_shapes=[pltpu.VMEM((16 * rows, depth), jnp.bfloat16)],
        ),
        compiler_params=pltpu.CompilerParams(vmem_limit_bytes=VMEM_BYTES),
        name="project",
    )(place, *blocks, *weights)


def per_device(
    queries,
    prefix_keys,
    prefix_values,
    cache_keys,
    cache_values,
    new_keys,
    new_values,
    suffix_len,
    out_weight,
):
    local = queries.shape[1]
    count = prefix_keys.shape[0]
    q = queries.reshape(2 * local, HEADS * HD)

    early = lax.all_gather(out_weight[:EARLY], Y, axis=0, tiled=False)
    q_parts = [q] + [lax.ppermute(q, Y, partner(4, k)) for k in (1, 2, 3)]

    split = [
        jnp.swapaxes(rows.reshape(count, 8, HD), 0, 1) for rows in (prefix_keys, prefix_values)
    ]
    own = lax.all_to_all(jnp.concatenate(split, axis=1), HEAD, 0, 0, tiled=True)
    held = []
    for step, blocks in enumerate(ring(own), 1):
        if step == 2:
            near = jnp.concatenate([blocks[offset] for offset in (0, -1, 1, -2, 2)], axis=0)
            held += [near, swap(near)]
        if step == 4:
            far = jnp.concatenate([blocks[offset] for offset in (-3, 3, -4)], axis=0)
            held += [far, swap(far)]

    parts = [None] * 4
    for k in (2, 3, 1, 0):
        message = attend(q_parts[k], held)
        parts[k] = message if k == 0 else lax.ppermute(message, Y, partner(4, k))

    suffix_keys = jnp.stack(
        [cache_keys[:, 0], cache_keys[:, 1], new_keys[0], new_keys[1]], axis=0
    ).astype(jnp.float32)
    suffix_values = jnp.stack(
        [cache_values[:, 0], cache_values[:, 1], new_values[0], new_values[1]], axis=0
    ).astype(jnp.float32)
    attended = combine(q, suffix_keys, suffix_values, suffix_len.reshape(local, 1), parts)

    late = lax.all_gather(after(out_weight[EARLY:], attended, early), Y, axis=0, tiled=False)

    for step, blocks in enumerate(ring(attended), 1):
        if step == 3:
            near = swap(jnp.concatenate([blocks[offset] for offset in (-2, -1, 0, 1, 2)], axis=0))
    far = swap(jnp.concatenate([blocks[offset] for offset in (3, -4, -3)], axis=0))
    place = jnp.stack([lax.rem(lax.axis_index("z") + 6, 8), lax.axis_index("c")]).astype(jnp.int32)
    order = (-2, -1, 0, 1, 2, 3, -4, -3)
    terms = project(place, [blocks[offset] for offset in order] + [near, far], [early, late])

    rows, cols = terms.shape[3:]
    arrived = lax.all_to_all(
        terms.reshape(32, 2 * rows, cols), Y + HEAD, 0, 0, tiled=True
    ).reshape(4, 8, 2, 2, local, cols)
    summed = jnp.sum(arrived.astype(jnp.float32), axis=1).astype(jnp.bfloat16)
    return jnp.transpose(summed, (2, 0, 1, 3, 4)).reshape(2, 8 * local, cols)


def solution(mesh):
    split_mesh = Mesh(mesh.devices.reshape(8, 2, 2, 2, 4, 2), SEQ + HEAD)
    in_specs = (
        P(None, SEQ, HEAD),
        P(SEQ + HEAD, None),
        P(SEQ + HEAD, None),
        P(SEQ, None, HEAD),
        P(SEQ, None, HEAD),
        P(None, SEQ, HEAD),
        P(None, SEQ, HEAD),
        P(SEQ),
        P(HEAD, SEQ),
    )
    out_specs = P(None, HEAD, SEQ)
    return jax.shard_map(
        per_device, mesh=split_mesh, in_specs=in_specs, out_specs=out_specs, check_vma=False
    )
```

time: 286 us -> 197 us (0.69)
  waiting for transfers between devices: 107 us -> 18.8 us
  blocking collectives: 85.5 us -> 37.3 us
  starting transfers between devices: 50.5 us -> 98.3 us
  Pallas kernels: 25.7 us -> 17.5 us
  local copies, waits for them, and re-layouts: 2.78 us -> 8.64 us
    all_gather x1 -> x2, waiting for transfers between devices: 93.5 us -> 0.01 us  [the longest x1 0.01 us: per_device(): early = lax.all_gather(out_weight[:EARLY], Y, axis=0, tiled=False)]
    all_to_all x2 -> x1, blocking collectives: 85.5 us -> 37.3 us  [per_device(): lax.all_to_all(terms.reshape(32, 2 * rows, cols), Y + HEAD, 0, 0, tiled=T...]
    ppermute x15 -> x24, starting transfers between devices: 50.5 us -> 89.9 us  [the longest x6 30.2 us: ring(): down = lax.ppermute(down, 'z', shift(8, -1))]
    all_to_all x0 -> x1, starting transfers between devices: none -> 8.38 us  [per_device(): own = lax.all_to_all(jnp.concatenate(split, axis=1), HEAD, 0, 0, tiled=True)]
    pallas_call x4, Pallas kernels: 18.6 us -> 11.3 us  [attend(): pl.pallas_call(attention_kernel, out_shape=jax.ShapeDtypeStruct((rows, HE...]
    ppermute x15 -> x24, waiting for transfers between devices: 12.5 us -> 17.5 us  [the longest x8 9.91 us: ring(): up = lax.ppermute(up, 'z', shift(8, 1))]
    slice x0 -> x2, local copies, waits for them, and re-layouts: none -> 3.83 us  [the longest x1 2.04 us: per_device(): early = lax.all_gather(out_weight[:EARLY], Y, axis=0, tiled=False)]
  transfers between devices with their start and end apart: 16 -> 27, of which waited for: 6 -> 8; matrix products, arithmetic and copies ran while one was open for 1% -> 2% of each run, Pallas kernels for 7% -> 6%
where the time goes in v2:
time: 197 us; the launch traced here: 196 us
  starting transfers between devices  98.3 us (50%)
  blocking collectives  37.3 us (19%)
  waiting for transfers between devices  18.8 us (10%)
  Pallas kernels  17.5 us (9%)
  between operations  14 us (7%)
  local copies, waits for them, and re-layouts  8.64 us (4%)
    all_to_all x1, blocking collectives, per_device(): lax.all_to_all(terms.reshape(32, 2 * rows, cols), Y + HEAD, 0, 0, tiled=T...  37.3 us
    ppermute x6, starting transfers between devices, ring(): down = lax.ppermute(down, 'z', shift(8, -1))  30.2 us
    ppermute x4, starting transfers between devices, swap(): return lax.ppermute(value, 'c', partner(2, 1))  25.4 us
    ppermute x8, starting transfers between devices, ring(): up = lax.ppermute(up, 'z', shift(8, 1))  16.8 us
    pallas_call x4, Pallas kernels, attend(): pl.pallas_call(attention_kernel, out_shape=jax.ShapeDtypeStruct((rows, HE...  11.3 us
    ppermute x8, waiting for transfers between devices, ring(): up = lax.ppermute(up, 'z', shift(8, 1))  9.91 us
    ppermute x3, starting transfers between devices, per_device(): q_parts = [q] + [lax.ppermute(q, Y, partner(4, k)) for k in (1, 2, 3)]  8.89 us
    ppermute x3, starting transfers between devices, per_device(): parts[k] = message if k == 0 else lax.ppermute(message, Y, partner(4, k))  8.69 us
  transfers between devices with their start and end apart: 27, of which 8 were waited for; matrix products, arithmetic and copies ran while one was open for 2% of the time, Pallas kernels for 6%

profile of v2, /device:TPU:9, one launch (start us, length us, event | category | flops | bytes accessed | tf_op | source)
XLA Modules:
  0.0 195.5 jit_solution(13370493307224475528)
XLA Ops:
  6.5 0.0 all-gather.5.cloned.1.call-start
  6.6 2.0 %slice.28 = bf16[1280,256]{1,0:T(8,128)(2,1)} slice(bf16[2048,256]{1,0:T(8,128)(2,1)} %param.17), slice={[0:1280], [0:256]} | slice | bytes 1310720 | tf_op jit(solution)/shard_map/slice | solution.py:228
  8.6 0.0 all-gather.5.cloned.1.call-update
  8.7 0.9 bitcast_bitcast_fusion
  9.5 0.7 pad_maximum_fusion.1
  10.2 8.4 %all-to-all-start = ((bf16[8,64,128]{2,1,0:T(8,128)(2,1)}), bf16[8,64,128]{2,1,0:T(8,128)(2,1)S(1)}, u32[]{:S(2)}, u32[]{:S(2)}) async-start(bf16[8,64,128]{2,1,0:T(8,128)(2,1)} %pad_maximum_fusion.1), calls=%async_computation | async-start | bytes 262144 | tf_op jit(solution)/shard_map/all_to_all | solution.py:234
  18.6 0.0 all-gather.7.cloned.1.call-start
  18.6 2.3 %collective-permute-start.13 = (bf16[32,2048]{1,0:T(8,128)(2,1)S(1)}, bf16[32,2048]{1,0:T(8,128)(2,1)S(1)}, u32[]{:S(2)}, u32[]{:S(2)}) collective-permute-start(bf16[32,2048]{1,0:T(8,128)(2,1)S(1)} %bitcast.34), channel_id=1, source_target_pairs={{0,48},{16,32},{32,16},{48,0},{1,49},{17,33},{33,17},{49,1},{2,50}... | collective-permute-start | bytes 393224 | tf_op jit(solution)/shard_map/ppermute | solution.py:229
  20.9 4.7 %collective-permute-start.11 = (bf16[32,2048]{1,0:T(8,128)(2,1)S(1)}, bf16[32,2048]{1,0:T(8,128)(2,1)S(1)}, u32[]{:S(2)}, u32[]{:S(2)}) collective-permute-start(bf16[32,2048]{1,0:T(8,128)(2,1)S(1)} %bitcast.35), channel_id=1, source_target_pairs={{0,32},{16,48},{32,0},{48,16},{1,33},{17,49},{33,1},{49,17},{2,34}... | collective-permute-start | bytes 393224 | tf_op jit(solution)/shard_map/ppermute | solution.py:229
  25.6 1.9 collective-permute-start.9
  27.6 1.3 all-to-all-done
  28.8 10.7 %collective-permute-start.1 = (bf16[8,64,128]{2,1,0:T(8,128)(2,1)S(1)}, bf16[8,64,128]{2,1,0:T(8,128)(2,1)S(1)}, u32[]{:S(2)}, u32[]{:S(2)}) collective-permute-start(bf16[8,64,128]{2,1,0:T(8,128)(2,1)S(1)} %all-to-all-done), channel_id=1, source_target_pairs={{0,448},{64,0},{128,64},{192,128},{256,192},{320,256},{384,320},{4... | collective-permute-start | bytes 393224 | tf_op jit(solution)/shard_map/ppermute | solution.py:40
  39.5 1.9 collective-permute-start
  41.5 0.0 collective-permute-done.1
  41.5 5.1 %collective-permute-start.3 = (bf16[8,64,128]{2,1,0:T(8,128)(2,1)S(1)}, bf16[8,64,128]{2,1,0:T(8,128)(2,1)S(1)}, u32[]{:S(2)}, u32[]{:S(2)}) collective-permute-start(bf16[8,64,128]{2,1,0:T(8,128)(2,1)S(1)} %collective-permute-done.1), channel_id=1, source_target_pairs={{0,448},{64,0},{128,64},{192,128},{256,192},{320,256},{384,320},{4... | collective-permute-start | bytes 393224 | tf_op jit(solution)/shard_map/ppermute | solution.py:40
  46.5 0.0 collective-permute-done
  46.6 1.9 collective-permute-start.2
  48.5 0.0 collective-permute-done.3
  48.6 4.9 %collective-permute-start.6 = (bf16[8,64,128]{2,1,0:T(8,128)(2,1)S(1)}, bf16[8,64,128]{2,1,0:T(8,128)(2,1)S(1)}, u32[]{:S(2)}, u32[]{:S(2)}) collective-permute-start(bf16[8,64,128]{2,1,0:T(8,128)(2,1)S(1)} %collective-permute-done.3), channel_id=1, source_target_pairs={{0,448},{64,0},{128,64},{192,128},{256,192},{320,256},{384,320},{4... | collective-permute-start | bytes 393224 | tf_op jit(solution)/shard_map/ppermute | solution.py:40
  53.5 0.0 collective-permute-done.2
  53.5 1.9 collective-permute-start.5
  55.5 4.9 %collective-permute-done.5 = bf16[8,64,128]{2,1,0:T(8,128)(2,1)S(1)} collective-permute-done((bf16[8,64,128]{2,1,0:T(8,128)(2,1)S(1)}, bf16[8,64,128]{2,1,0:T(8,128)(2,1)S(1)}, u32[]{:S(2)}, u32[]{:S(2)}) %collective-permute-start.5) | collective-permute-done | bytes 131104 | tf_op jit(solution)/shard_map/ppermute | solution.py:37
  60.4 1.9 collective-permute-start.7
  62.3 7.6 %collective-permute-start.4 = (bf16[40,64,128]{2,1,0:T(8,128)(2,1)S(1)}, bf16[40,64,128]{2,1,0:T(8,128)(2,1)S(1)}, u32[]{:S(2)}, u32[]{:S(2)}) collective-permute-start(bf16[40,64,128]{2,1,0:T(8,128)(2,1)S(1)} %constant_dynamic-update-slice_fusion.refs_0_), channel_id=1, source_target_pairs={{0,8},{8,0},{1,9},{9,1},{2,10},{10,2},{3,11},{11,3},{4,12},{12,4},... | collective-permute-start | bytes 1966088 | tf_op jit(solution)/shard_map/ppermute | solution.py:46
  70.0 6.1 %collective-permute-start.8 = (bf16[24,64,128]{2,1,0:T(8,128)(2,1)S(1)}, bf16[24,64,128]{2,1,0:T(8,128)(2,1)S(1)}, u32[]{:S(2)}, u32[]{:S(2)}) collective-permute-start(bf16[24,64,128]{2,1,0:T(8,128)(2,1)S(1)} %constant_dynamic-update-slice_fusion.5.refs_2_), channel_id=1, source_target_pairs={{0,8},{8,0},{1,9},{9,1},{2,10},{10,2},{3,11},{11,3},{4,12},{12,4},... | collective-permute-start | bytes 1179656 | tf_op jit(solution)/shard_map/ppermute | solution.py:46
  76.1 1.3 collective-permute-done.8.refs_3_
  77.4 2.8 %attend.5 = bf16[32,2176]{1,0:T(8,128)(2,1)S(1)} custom-call(bf16[32,2048]{1,0:T(8,128)(2,1)S(1)} %collective-permute-done.9.q_ref, bf16[40,64,128]{2,1,0:T(8,128)(2,1)S(1)} %constant_dynamic-update-slice_fusion.refs_0_, bf16[40,64,128]{2,1,0:T(8,128)(2,1)S(1)} %collective-permute-done.4.refs_1_, ...), custom_call_target="tpu_custom_call" | custom-call | tf_op jit(solution)/shard_map/attend/pallas_call | solution.py:105
  80.2 0.0 copy-start.7
  80.3 0.0 copy-start.9
  80.3 0.0 copy-start.8
  80.3 2.4 %collective-permute-start.10 = (bf16[32,2176]{1,0:T(8,128)(2,1)S(1)}, bf16[32,2176]{1,0:T(8,128)(2,1)S(1)}, u32[]{:S(2)}, u32[]{:S(2)}) collective-permute-start(bf16[32,2176]{1,0:T(8,128)(2,1)S(1)} %attend.5), channel_id=1, source_target_pairs={{0,16},{16,0},{32,48},{48,32},{1,17},{17,1},{33,49},{49,33},{2,18}... | collective-permute-start | bytes 417800 | tf_op jit(solution)/shard_map/ppermute | solution.py:247
  82.7 2.8 %attend.6 = bf16[32,2176]{1,0:T(8,128)(2,1)S(1)} custom-call(bf16[32,2048]{1,0:T(8,128)(2,1)S(1)} %collective-permute-done.11.q_ref, bf16[40,64,128]{2,1,0:T(8,128)(2,1)S(1)} %constant_dynamic-update-slice_fusion.refs_0_, bf16[40,64,128]{2,1,0:T(8,128)(2,1)S(1)} %collective-permute-done.4.refs_1_, ...), custom_call_target="tpu_custom_call" | custom-call | tf_op jit(solution)/shard_map/attend/pallas_call | solution.py:105
  85.5 3.2 %collective-permute-start.12 = (bf16[32,2176]{1,0:T(8,128)(2,1)S(1)}, bf16[32,2176]{1,0:T(8,128)(2,1)S(1)}, u32[]{:S(2)}, u32[]{:S(2)}) collective-permute-start(bf16[32,2176]{1,0:T(8,128)(2,1)S(1)} %attend.6), channel_id=1, source_target_pairs={{0,32},{16,48},{32,0},{48,16},{1,33},{17,49},{33,1},{49,17},{2,34}... | collective-permute-start | bytes 417800 | tf_op jit(solution)/shard_map/ppermute | solution.py:247
  88.8 2.8 %attend.7 = bf16[32,2176]{1,0:T(8,128)(2,1)S(1)} custom-call(bf16[32,2048]{1,0:T(8,128)(2,1)S(1)} %collective-permute-done.13.q_ref, bf16[40,64,128]{2,1,0:T(8,128)(2,1)S(1)} %constant_dynamic-update-slice_fusion.refs_0_, bf16[40,64,128]{2,1,0:T(8,128)(2,1)S(1)} %collective-permute-done.4.refs_1_, ...), custom_call_target="tpu_custom_call" | custom-call | tf_op jit(solution)/shard_map/attend/pallas_call | solution.py:105
  91.6 3.0 %collective-permute-start.14 = (bf16[32,2176]{1,0:T(8,128)(2,1)S(1)}, bf16[32,2176]{1,0:T(8,128)(2,1)S(1)}, u32[]{:S(2)}, u32[]{:S(2)}) collective-permute-start(bf16[32,2176]{1,0:T(8,128)(2,1)S(1)} %attend.7), channel_id=1, source_target_pairs={{0,48},{16,32},{32,16},{48,0},{1,49},{17,33},{33,17},{49,1},{2,50}... | collective-permute-start | bytes 417800 | tf_op jit(solution)/shard_map/ppermute | solution.py:247
  94.7 1.8 slice.29.refs_0_
  96.5 0.1 copy.36.len_ref
  96.6 2.8 %attend.4.m0_ref = bf16[32,2176]{1,0:T(8,128)(2,1)S(1)} custom-call(bf16[32,2048]{1,0:T(8,128)(2,1)S(1)} %bitcast.37, bf16[40,64,128]{2,1,0:T(8,128)(2,1)S(1)} %constant_dynamic-update-slice_fusion.refs_0_, bf16[40,64,128]{2,1,0:T(8,128)(2,1)S(1)} %collective-permute-done.4.refs_1_, bf16[24,64,128]{2,1,0:T(8,128)(2,1)S(1)} %constant_dynamic-update-slice_fusion.5.refs_2_, ...), custom_call_target="tpu_custom_call" | custom-call | tf_op jit(solution)/shard_map/attend/pallas_call | solution.py:105
  99.5 3.3 %collective-permute-done.14.m3_ref = bf16[32,2176]{1,0:T(8,128)(2,1)S(1)} collective-permute-done((bf16[32,2176]{1,0:T(8,128)(2,1)S(1)}, bf16[32,2176]{1,0:T(8,128)(2,1)S(1)}, u32[]{:S(2)}, u32[]{:S(2)}) %collective-permute-start.14) | collective-permute-done | bytes 139296 | tf_op jit(solution)/shard_map/ppermute | solution.py:247
  102.7 1.0 combine.1.refs_1_.refs_2_
  103.8 0.0 copy-start.1
  103.8 0.6 copy-done.1
  104.4 0.0 all-gather.7.cloned.1.call-update
  104.5 0.9 copy-done.2
  105.3 1.9 collective-permute-start.17
  107.2 3.4 %collective-permute-start.15 = (bf16[32,2048]{1,0:T(8,128)(2,1)S(1)}, bf16[32,2048]{1,0:T(8,128)(2,1)S(1)}, u32[]{:S(2)}, u32[]{:S(2)}) collective-permute-start(bf16[32,2048]{1,0:T(8,128)(2,1)S(1)} %copy-done.2), channel_id=1, source_target_pairs={{0,64},{64,128},{128,192},{192,256},{256,320},{320,384},{384,448},... | collective-permute-start | bytes 393224 | tf_op jit(solution)/shard_map/ppermute | solution.py:37
  110.6 1.1 collective-permute-done.17.refs_3_
  111.7 3.4 %collective-permute-start.18 = (bf16[32,2048]{1,0:T(8,128)(2,1)S(1)}, bf16[32,2048]{1,0:T(8,128)(2,1)S(1)}, u32[]{:S(2)}, u32[]{:S(2)}) collective-permute-start(bf16[32,2048]{1,0:T(8,128)(2,1)S(1)} %collective-permute-done.17.refs_3_), channel_id=1, source_target_pairs={{0,448},{64,0},{128,64},{192,128},{256,192},{320,256},{384,320},{4... | collective-permute-start | bytes 393224 | tf_op jit(solution)/shard_map/ppermute | solution.py:40
  115.1 1.9 collective-permute-start.16
  117.1 0.7 collective-permute-done.18.refs_4_
  117.8 4.2 %collective-permute-start.19 = (bf16[32,2048]{1,0:T(8,128)(2,1)S(1)}, bf16[32,2048]{1,0:T(8,128)(2,1)S(1)}, u32[]{:S(2)}, u32[]{:S(2)}) collective-permute-start(bf16[32,2048]{1,0:T(8,128)(2,1)S(1)} %collective-permute-done.18.refs_4_), channel_id=1, source_target_pairs={{0,448},{64,0},{128,64},{192,128},{256,192},{320,256},{384,320},{4... | collective-permute-start | bytes 393224 | tf_op jit(solution)/shard_map/ppermute | solution.py:40
  122.0 0.0 collective-permute-done.16.refs_0_
  122.1 1.9 collective-permute-start.20
  124.1 4.9 %collective-permute-done.20.refs_7_ = bf16[32,2048]{1,0:T(8,128)(2,1)S(1)} collective-permute-done((bf16[32,2048]{1,0:T(8,128)(2,1)S(1)}, bf16[32,2048]{1,0:T(8,128)(2,1)S(1)}, u32[]{:S(2)}, u32[]{:S(2)}) %collective-permute-start.20) | collective-permute-done | bytes 131104 | tf_op jit(solution)/shard_map/ppermute | solution.py:37
  129.0 1.9 collective-permute-start.21
  130.9 5.6 %collective-permute-start.22 = (bf16[160,2048]{1,0:T(8,128)(2,1)S(1)}, bf16[160,2048]{1,0:T(8,128)(2,1)S(1)}, u32[]{:S(2)}, u32[]{:S(2)}) collective-permute-start(bf16[160,2048]{1,0:T(8,128)(2,1)S(1)} %constant_dynamic-update-slice_fusion.8), channel_id=1, source_target_pairs={{0,8},{8,0},{1,9},{9,1},{2,10},{10,2},{3,11},{11,3},{4,12},{12,4},... | collective-permute-start | bytes 1966088 | tf_op jit(solution)/shard_map/ppermute | solution.py:46
  136.6 6.1 %collective-permute-start.23 = (bf16[96,2048]{1,0:T(8,128)(2,1)S(1)}, bf16[96,2048]{1,0:T(8,128)(2,1)S(1)}, u32[]{:S(2)}, u32[]{:S(2)}) collective-permute-start(bf16[96,2048]{1,0:T(8,128)(2,1)S(1)} %pad_maximum_fusion), channel_id=1, source_target_pairs={{0,8},{8,0},{1,9},{9,1},{2,10},{10,2},{3,11},{11,3},{4,12},{12,4},... | collective-permute-start | bytes 1179656 | tf_op jit(solution)/shard_map/ppermute | solution.py:46
  142.7 0.1 pad_add_fusion.place_ref
  142.8 1.2 collective-permute-done.23.refs_9_
  144.0 1.4 copy-done.3
  145.4 5.1 %project.1 = bf16[4,8,2,32,256]{4,3,2,1,0:T(8,128)(2,1)S(1)} custom-call(s32[2]{0:T(128)S(1)} %pad_add_fusion.place_ref, bf16[32,2048]{1,0:T(8,128)(2,1)S(1)} %collective-permute-done.16.refs_0_, bf16[32,2048]{1,0:T(8,128)(2,1)S(1)} %collective-permute-done.15.refs_1_, bf16[32,2048]{1,0:T(8,128)(2,1)S(1)} %copy-done.2, ...), custom_call_target="tpu_custom_call" | custom-call | tf_op jit(solution)/shard_map/project/pallas_call | solution.py:197
  150.5 37.3 %all_to_all.10 = bf16[32,64,256]{2,1,0:T(8,128)(2,1)S(1)} all-to-all(bf16[32,64,256]{2,1,0:T(8,128)(2,1)S(1)} %bitcast.32), channel_id=1, replica_groups=mesh['z'=8,'u'=2,'v'=2,'c'=2,'x'=4,'w'=2] {'u','v','x','w'}, dimensions={0} | all-to-all | bytes 2097152 | tf_op jit(solution)/shard_map/all_to_all | solution.py:268
  187.8 0.2 reduce_sum.12
  188.0 0.7 copy.37
  (48 shorter events, 0.3 us)
Async XLA Ops:
  6.5 2.1 %copy-start = (bf16[32,1024]{1,0:T(8,128)(2,1)S(1)}, bf16[32,1024]{1,0:T(8,128)(2,1)}, u32[]{:S(2)}) copy-start(bf16[32,1024]{1,0:T(8,128)(2,1)} %param.10) | copy-start | bytes 196612
  6.5 12.1 %copy-start.4 = (bf16[2,16,2048]{2,1,0:T(8,128)(2,1)S(1)}, bf16[2,16,2048]{2,1,0:T(8,128)(2,1)}, u32[]{:S(2)}) copy-start(bf16[2,16,2048]{2,1,0:T(8,128)(2,1)} %param.9) | copy-start | bytes 393220
  6.5 21.0 %copy-start.5 = (bf16[16,2,128]{2,1,0:T(2,128)(2,1)S(1)}, bf16[16,2,128]{2,1,0:T(2,128)(2,1)}, u32[]{:S(2)}) copy-start(bf16[16,2,128]{2,1,0:T(2,128)(2,1)} %param.12) | copy-start | bytes 24580
  6.5 34.9 %copy-start.6 = (bf16[16,2,128]{2,1,0:T(2,128)(2,1)S(1)}, bf16[16,2,128]{2,1,0:T(2,128)(2,1)}, u32[]{:S(2)}) copy-start(bf16[16,2,128]{2,1,0:T(2,128)(2,1)} %param.13) | copy-start | bytes 24580
  6.5 97.9 %all-gather.5.cloned.1.call-start = ((), (), s32[]{:S(2)}) async-start(), calls=%async_computation.2 | async-start | bytes 3276800 | tf_op jit(solution)/shard_map/all_gather | solution.py:228
  10.2 18.6 %all-to-all-start = ((bf16[8,64,128]{2,1,0:T(8,128)(2,1)}), bf16[8,64,128]{2,1,0:T(8,128)(2,1)S(1)}, u32[]{:S(2)}, u32[]{:S(2)}) async-start(bf16[8,64,128]{2,1,0:T(8,128)(2,1)} %pad_maximum_fusion.1), calls=%async_computation | async-start | bytes 262144 | tf_op jit(solution)/shard_map/all_to_all | solution.py:234
  18.6 125.4 %all-gather.7.cloned.1.call-start = ((), (), s32[]{:S(2)}) async-start(), calls=%async_computation.3 | async-start | bytes 1966080 | tf_op jit(solution)/shard_map/all_gather | solution.py:257
  18.6 70.2 %collective-permute-start.13 = (bf16[32,2048]{1,0:T(8,128)(2,1)S(1)}, bf16[32,2048]{1,0:T(8,128)(2,1)S(1)}, u32[]{:S(2)}, u32[]{:S(2)}) collective-permute-start(bf16[32,2048]{1,0:T(8,128)(2,1)S(1)} %bitcast.34), channel_id=1, source_target_pairs={{0,48},{16,32},{32,16},{48,0},{1,49},{17,33},{33,17},{49,1},{2,50}... | collective-permute-start | bytes 393224 | tf_op jit(solution)/shard_map/ppermute | solution.py:229
  20.9 61.8 %collective-permute-start.11 = (bf16[32,2048]{1,0:T(8,128)(2,1)S(1)}, bf16[32,2048]{1,0:T(8,128)(2,1)S(1)}, u32[]{:S(2)}, u32[]{:S(2)}) collective-permute-start(bf16[32,2048]{1,0:T(8,128)(2,1)S(1)} %bitcast.35), channel_id=1, source_target_pairs={{0,32},{16,48},{32,0},{48,16},{1,33},{17,49},{33,1},{49,17},{2,34}... | collective-permute-start | bytes 393224 | tf_op jit(solution)/shard_map/ppermute | solution.py:229
  25.6 50.5 %collective-permute-start.9 = (bf16[32,2048]{1,0:T(8,128)(2,1)S(1)}, bf16[32,2048]{1,0:T(8,128)(2,1)S(1)}, u32[]{:S(2)}, u32[]{:S(2)}) collective-permute-start(bf16[32,2048]{1,0:T(8,128)(2,1)S(1)} %bitcast.36), channel_id=1, source_target_pairs={{0,16},{16,0},{32,48},{48,32},{1,17},{17,1},{33,49},{49,33},{2,18}... | collective-permute-start | bytes 393224 | tf_op jit(solution)/shard_map/ppermute | solution.py:229
  28.8 12.6 %collective-permute-start.1 = (bf16[8,64,128]{2,1,0:T(8,128)(2,1)S(1)}, bf16[8,64,128]{2,1,0:T(8,128)(2,1)S(1)}, u32[]{:S(2)}, u32[]{:S(2)}) collective-permute-start(bf16[8,64,128]{2,1,0:T(8,128)(2,1)S(1)} %all-to-all-done), channel_id=1, source_target_pairs={{0,448},{64,0},{128,64},{192,128},{256,192},{320,256},{384,320},{4... | collective-permute-start | bytes 393224 | tf_op jit(solution)/shard_map/ppermute | solution.py:40
  39.5 7.1 %collective-permute-start = (bf16[8,64,128]{2,1,0:T(8,128)(2,1)S(1)}, bf16[8,64,128]{2,1,0:T(8,128)(2,1)S(1)}, u32[]{:S(2)}, u32[]{:S(2)}) collective-permute-start(bf16[8,64,128]{2,1,0:T(8,128)(2,1)S(1)} %all-to-all-done), channel_id=1, source_target_pairs={{0,64},{64,128},{128,192},{192,256},{256,320},{320,384},{384,448},... | collective-permute-start | bytes 393224 | tf_op jit(solution)/shard_map/ppermute | solution.py:37
  41.5 7.1 %collective-permute-start.3 = (bf16[8,64,128]{2,1,0:T(8,128)(2,1)S(1)}, bf16[8,64,128]{2,1,0:T(8,128)(2,1)S(1)}, u32[]{:S(2)}, u32[]{:S(2)}) collective-permute-start(bf16[8,64,128]{2,1,0:T(8,128)(2,1)S(1)} %collective-permute-done.1), channel_id=1, source_target_pairs={{0,448},{64,0},{128,64},{192,128},{256,192},{320,256},{384,320},{4... | collective-permute-start | bytes 393224 | tf_op jit(solution)/shard_map/ppermute | solution.py:40
  46.6 6.9 %collective-permute-start.2 = (bf16[8,64,128]{2,1,0:T(8,128)(2,1)S(1)}, bf16[8,64,128]{2,1,0:T(8,128)(2,1)S(1)}, u32[]{:S(2)}, u32[]{:S(2)}) collective-permute-start(bf16[8,64,128]{2,1,0:T(8,128)(2,1)S(1)} %collective-permute-done), channel_id=1, source_target_pairs={{0,64},{64,128},{128,192},{192,256},{256,320},{320,384},{384,448},... | collective-permute-start | bytes 393224 | tf_op jit(solution)/shard_map/ppermute | solution.py:37
  48.6 13.8 %collective-permute-start.6 = (bf16[8,64,128]{2,1,0:T(8,128)(2,1)S(1)}, bf16[8,64,128]{2,1,0:T(8,128)(2,1)S(1)}, u32[]{:S(2)}, u32[]{:S(2)}) collective-permute-start(bf16[8,64,128]{2,1,0:T(8,128)(2,1)S(1)} %collective-permute-done.3), channel_id=1, source_target_pairs={{0,448},{64,0},{128,64},{192,128},{256,192},{320,256},{384,320},{4... | collective-permute-start | bytes 393224 | tf_op jit(solution)/shard_map/ppermute | solution.py:40
  53.5 6.9 %collective-permute-start.5 = (bf16[8,64,128]{2,1,0:T(8,128)(2,1)S(1)}, bf16[8,64,128]{2,1,0:T(8,128)(2,1)S(1)}, u32[]{:S(2)}, u32[]{:S(2)}) collective-permute-start(bf16[8,64,128]{2,1,0:T(8,128)(2,1)S(1)} %collective-permute-done.2), channel_id=1, source_target_pairs={{0,64},{64,128},{128,192},{192,256},{256,320},{320,384},{384,448},... | collective-permute-start | bytes 393224 | tf_op jit(solution)/shard_map/ppermute | solution.py:37
  60.4 9.6 %collective-permute-start.7 = (bf16[8,64,128]{2,1,0:T(8,128)(2,1)S(1)}, bf16[8,64,128]{2,1,0:T(8,128)(2,1)S(1)}, u32[]{:S(2)}, u32[]{:S(2)}) collective-permute-start(bf16[8,64,128]{2,1,0:T(8,128)(2,1)S(1)} %collective-permute-done.5), channel_id=1, source_target_pairs={{0,64},{64,128},{128,192},{192,256},{256,320},{320,384},{384,448},... | collective-permute-start | bytes 393224 | tf_op jit(solution)/shard_map/ppermute | solution.py:37
  62.3 15.1 %collective-permute-start.4 = (bf16[40,64,128]{2,1,0:T(8,128)(2,1)S(1)}, bf16[40,64,128]{2,1,0:T(8,128)(2,1)S(1)}, u32[]{:S(2)}, u32[]{:S(2)}) collective-permute-start(bf16[40,64,128]{2,1,0:T(8,128)(2,1)S(1)} %constant_dynamic-update-slice_fusion.refs_0_), channel_id=1, source_target_pairs={{0,8},{8,0},{1,9},{9,1},{2,10},{10,2},{3,11},{11,3},{4,12},{12,4},... | collective-permute-start | bytes 1966088 | tf_op jit(solution)/shard_map/ppermute | solution.py:46
  70.0 7.4 %collective-permute-start.8 = (bf16[24,64,128]{2,1,0:T(8,128)(2,1)S(1)}, bf16[24,64,128]{2,1,0:T(8,128)(2,1)S(1)}, u32[]{:S(2)}, u32[]{:S(2)}) collective-permute-start(bf16[24,64,128]{2,1,0:T(8,128)(2,1)S(1)} %constant_dynamic-update-slice_fusion.5.refs_2_), channel_id=1, source_target_pairs={{0,8},{8,0},{1,9},{9,1},{2,10},{10,2},{3,11},{11,3},{4,12},{12,4},... | collective-permute-start | bytes 1179656 | tf_op jit(solution)/shard_map/ppermute | solution.py:46
  80.2 14.4 %copy-start.7 = (bf16[2,16,128]{2,1,0:T(8,128)(2,1)S(1)}, bf16[2,16,128]{2,1,0:T(8,128)(2,1)}, u32[]{:S(2)}) copy-start(bf16[2,16,128]{2,1,0:T(8,128)(2,1)} %param.15) | copy-start | bytes 24580
  80.3 16.2 %copy-start.9 = (s32[16]{0:T(128)S(1)}, s32[16]{0:T(128)}, u32[]{:S(2)}) copy-start(s32[16]{0:T(128)} %param.16) | copy-start | bytes 196
  80.3 16.3 %copy-start.8 = (bf16[2,16,128]{2,1,0:T(8,128)(2,1)S(1)}, bf16[2,16,128]{2,1,0:T(8,128)(2,1)}, u32[]{:S(2)}) copy-start(bf16[2,16,128]{2,1,0:T(8,128)(2,1)} %param.14) | copy-start | bytes 24580
  80.3 19.2 %collective-permute-start.10 = (bf16[32,2176]{1,0:T(8,128)(2,1)S(1)}, bf16[32,2176]{1,0:T(8,128)(2,1)S(1)}, u32[]{:S(2)}, u32[]{:S(2)}) collective-permute-start(bf16[32,2176]{1,0:T(8,128)(2,1)S(1)} %attend.5), channel_id=1, source_target_pairs={{0,16},{16,0},{32,48},{48,32},{1,17},{17,1},{33,49},{49,33},{2,18}... | collective-permute-start | bytes 417800 | tf_op jit(solution)/shard_map/ppermute | solution.py:247
  85.5 13.9 %collective-permute-start.12 = (bf16[32,2176]{1,0:T(8,128)(2,1)S(1)}, bf16[32,2176]{1,0:T(8,128)(2,1)S(1)}, u32[]{:S(2)}, u32[]{:S(2)}) collective-permute-start(bf16[32,2176]{1,0:T(8,128)(2,1)S(1)} %attend.6), channel_id=1, source_target_pairs={{0,32},{16,48},{32,0},{48,16},{1,33},{17,49},{33,1},{49,17},{2,34}... | collective-permute-start | bytes 417800 | tf_op jit(solution)/shard_map/ppermute | solution.py:247
  91.6 11.1 %collective-permute-start.14 = (bf16[32,2176]{1,0:T(8,128)(2,1)S(1)}, bf16[32,2176]{1,0:T(8,128)(2,1)S(1)}, u32[]{:S(2)}, u32[]{:S(2)}) collective-permute-start(bf16[32,2176]{1,0:T(8,128)(2,1)S(1)} %attend.7), channel_id=1, source_target_pairs={{0,48},{16,32},{32,16},{48,0},{1,49},{17,33},{33,17},{49,1},{2,50}... | collective-permute-start | bytes 417800 | tf_op jit(solution)/shard_map/ppermute | solution.py:247
  103.8 0.7 copy-start.1
  104.4 0.9 copy-start.2
  105.3 6.4 %collective-permute-start.17 = (bf16[32,2048]{1,0:T(8,128)(2,1)S(1)}, bf16[32,2048]{1,0:T(8,128)(2,1)S(1)}, u32[]{:S(2)}, u32[]{:S(2)}) collective-permute-start(bf16[32,2048]{1,0:T(8,128)(2,1)S(1)} %copy-done.2), channel_id=1, source_target_pairs={{0,448},{64,0},{128,64},{192,128},{256,192},{320,256},{384,320},{4... | collective-permute-start | bytes 393224 | tf_op jit(solution)/shard_map/ppermute | solution.py:40
  107.2 7.9 %collective-permute-start.15 = (bf16[32,2048]{1,0:T(8,128)(2,1)S(1)}, bf16[32,2048]{1,0:T(8,128)(2,1)S(1)}, u32[]{:S(2)}, u32[]{:S(2)}) collective-permute-start(bf16[32,2048]{1,0:T(8,128)(2,1)S(1)} %copy-done.2), channel_id=1, source_target_pairs={{0,64},{64,128},{128,192},{192,256},{256,320},{320,384},{384,448},... | collective-permute-start | bytes 393224 | tf_op jit(solution)/shard_map/ppermute | solution.py:37
  111.7 6.1 %collective-permute-start.18 = (bf16[32,2048]{1,0:T(8,128)(2,1)S(1)}, bf16[32,2048]{1,0:T(8,128)(2,1)S(1)}, u32[]{:S(2)}, u32[]{:S(2)}) collective-permute-start(bf16[32,2048]{1,0:T(8,128)(2,1)S(1)} %collective-permute-done.17.refs_3_), channel_id=1, source_target_pairs={{0,448},{64,0},{128,64},{192,128},{256,192},{320,256},{384,320},{4... | collective-permute-start | bytes 393224 | tf_op jit(solution)/shard_map/ppermute | solution.py:40
  115.1 6.9 %collective-permute-start.16 = (bf16[32,2048]{1,0:T(8,128)(2,1)S(1)}, bf16[32,2048]{1,0:T(8,128)(2,1)S(1)}, u32[]{:S(2)}, u32[]{:S(2)}) collective-permute-start(bf16[32,2048]{1,0:T(8,128)(2,1)S(1)} %collective-permute-done.15.refs_1_), channel_id=1, source_target_pairs={{0,64},{64,128},{128,192},{192,256},{256,320},{320,384},{384,448},... | collective-permute-start | bytes 393224 | tf_op jit(solution)/shard_map/ppermute | solution.py:37
  117.8 18.7 %collective-permute-start.19 = (bf16[32,2048]{1,0:T(8,128)(2,1)S(1)}, bf16[32,2048]{1,0:T(8,128)(2,1)S(1)}, u32[]{:S(2)}, u32[]{:S(2)}) collective-permute-start(bf16[32,2048]{1,0:T(8,128)(2,1)S(1)} %collective-permute-done.18.refs_4_), channel_id=1, source_target_pairs={{0,448},{64,0},{128,64},{192,128},{256,192},{320,256},{384,320},{4... | collective-permute-start | bytes 393224 | tf_op jit(solution)/shard_map/ppermute | solution.py:40
  122.1 6.9 %collective-permute-start.20 = (bf16[32,2048]{1,0:T(8,128)(2,1)S(1)}, bf16[32,2048]{1,0:T(8,128)(2,1)S(1)}, u32[]{:S(2)}, u32[]{:S(2)}) collective-permute-start(bf16[32,2048]{1,0:T(8,128)(2,1)S(1)} %collective-permute-done.16.refs_0_), channel_id=1, source_target_pairs={{0,64},{64,128},{128,192},{192,256},{256,320},{320,384},{384,448},... | collective-permute-start | bytes 393224 | tf_op jit(solution)/shard_map/ppermute | solution.py:37
  129.0 7.6 %collective-permute-start.21 = (bf16[32,2048]{1,0:T(8,128)(2,1)S(1)}, bf16[32,2048]{1,0:T(8,128)(2,1)S(1)}, u32[]{:S(2)}, u32[]{:S(2)}) collective-permute-start(bf16[32,2048]{1,0:T(8,128)(2,1)S(1)} %collective-permute-done.20.refs_7_), channel_id=1, source_target_pairs={{0,64},{64,128},{128,192},{192,256},{256,320},{320,384},{384,448},... | collective-permute-start | bytes 393224 | tf_op jit(solution)/shard_map/ppermute | solution.py:37
  130.9 13.1 %collective-permute-start.22 = (bf16[160,2048]{1,0:T(8,128)(2,1)S(1)}, bf16[160,2048]{1,0:T(8,128)(2,1)S(1)}, u32[]{:S(2)}, u32[]{:S(2)}) collective-permute-start(bf16[160,2048]{1,0:T(8,128)(2,1)S(1)} %constant_dynamic-update-slice_fusion.8), channel_id=1, source_target_pairs={{0,8},{8,0},{1,9},{9,1},{2,10},{10,2},{3,11},{11,3},{4,12},{12,4},... | collective-permute-start | bytes 1966088 | tf_op jit(solution)/shard_map/ppermute | solution.py:46
  136.6 7.4 %collective-permute-start.23 = (bf16[96,2048]{1,0:T(8,128)(2,1)S(1)}, bf16[96,2048]{1,0:T(8,128)(2,1)S(1)}, u32[]{:S(2)}, u32[]{:S(2)}) collective-permute-start(bf16[96,2048]{1,0:T(8,128)(2,1)S(1)} %pad_maximum_fusion), channel_id=1, source_target_pairs={{0,8},{8,0},{1,9},{9,1},{2,10},{10,2},{3,11},{11,3},{4,12},{12,4},... | collective-permute-start | bytes 1179656 | tf_op jit(solution)/shard_map/ppermute | solution.py:46
  144.0 1.4 copy-start.3
Sparse Core Ops, SparseCore 0:
  9.5 68.8 all-gather.4
  104.6 37.8 all-gather.6

commit v3 on v2

--- a/solution.py
+++ b/solution.py
@@ -17,7 +17,6 @@
 HEAD = ("x", "w")
 SEQ = ("z", "u", "v", "c")
 CHUNK = 8
-EARLY = 1280
 VMEM_BYTES = 48 * 1024 * 1024
 
 
@@ -40,6 +39,11 @@
             down = lax.ppermute(down, "z", shift(8, -1))
             blocks[step] = down
         yield blocks
+
+
+def replicate(value):
+    sent = jnp.broadcast_to(value[None], (8,) + value.shape)
+    return lax.all_to_all(sent, "z", 0, 0, tiled=True)
 
 
 def swap(value):
@@ -163,51 +167,32 @@
     )(q, keys, values, lens, *parts)
 
 
-def project_kernel(place_ref, *refs):
-    blocks = refs[:-4]
-    early_ref, late_ref, out_ref, held = refs[-4:]
+def project_kernel(place_ref, own_ref, other_ref, *refs):
+    weights, out_ref = refs[:4], refs[4]
     rows = out_ref.shape[3]
-
-    @pl.when(pl.program_id(0) == 0)
-    def _():
-        start = 0
-        for block in blocks:
-            held[start : start + block.shape[0], :] = block[...]
-            start += block.shape[0]
-
-    first = place_ref[0]
-    core = place_ref[1]
-    depth = early_ref.shape[1]
-    terms = jnp.dot(held[:, :depth], early_ref[0], preferred_element_type=jnp.float32)
-    terms += jnp.dot(held[:, depth:], late_ref[0], preferred_element_type=jnp.float32)
-    terms = terms.astype(jnp.bfloat16)
-    for side in range(2):
-        which = core if side == 0 else 1 - core
-        for index in range(8):
-            where = lax.rem(first + index, 8)
-            start = (side * 8 + index) * rows
-            out_ref[0, where, which] = terms[start : start + rows]
+    core, me = place_ref[0], place_ref[1]
+    for index, weight in enumerate(weights):
+        column = lax.bitwise_xor(me, index)
+        for side, rows_ref in enumerate((own_ref, other_ref)):
+            terms = jnp.dot(rows_ref[...], weight[...], preferred_element_type=jnp.float32)
+            terms = terms.astype(jnp.bfloat16)
+            which = lax.bitwise_xor(core, side)
+            for z in range(8):
+                out_ref[column, z, which] = terms[z * rows : (z + 1) * rows]
 
 
 def project(place, blocks, weights):
-    depth = blocks[0].shape[1]
-    quarters, _, cols = weights[0].shape
-    rows = sum(block.shape[0] for block in blocks) // 16
-    whole = [pl.BlockSpec(block.shape, lambda i, place: (0, 0)) for block in blocks]
+    rows = blocks[0].shape[0] // 8
+    cols = weights[0].shape[1]
+    whole = list(blocks) + list(weights)
     return pl.pallas_call(
         project_kernel,
-        out_shape=jax.ShapeDtypeStruct((quarters, 8, 2, rows, cols), jnp.bfloat16),
-        grid_spec=pltpu.PrefetchScalarGridSpec(
-            num_scalar_prefetch=1,
-            grid=(quarters,),
-            in_specs=whole
-            + [pl.BlockSpec((1,) + part.shape[1:], lambda i, place: (i, 0, 0)) for part in weights],
-            out_specs=pl.BlockSpec((1, 8, 2, rows, cols), lambda i, place: (i, 0, 0, 0, 0)),
-            scratch_shapes=[pltpu.VMEM((16 * rows, depth), jnp.bfloat16)],
-        ),
+        out_shape=jax.ShapeDtypeStruct((4, 8, 2, rows, cols), jnp.bfloat16),
+        in_specs=[pl.BlockSpec(memory_space=pltpu.SMEM)]
+        + [pl.BlockSpec(memory_space=pltpu.VMEM)] * len(whole),
         compiler_params=pltpu.CompilerParams(vmem_limit_bytes=VMEM_BYTES),
         name="project",
-    )(place, *blocks, *weights)
+    )(place, *whole)
 
 
 def per_device(
@@ -225,20 +210,22 @@
     count = prefix_keys.shape[0]
     q = queries.reshape(2 * local, HEADS * HD)
 
-    early = lax.all_gather(out_weight[:EARLY], Y, axis=0, tiled=False)
     q_parts = [q] + [lax.ppermute(q, Y, partner(4, k)) for k in (1, 2, 3)]
 
     split = [
         jnp.swapaxes(rows.reshape(count, 8, HD), 0, 1) for rows in (prefix_keys, prefix_values)
     ]
     own = lax.all_to_all(jnp.concatenate(split, axis=1), HEAD, 0, 0, tiled=True)
+    weight_u = lax.ppermute(out_weight, "u", partner(2, 1))
+    weight_v = lax.ppermute(out_weight, "v", partner(2, 1))
     held = []
     for step, blocks in enumerate(ring(own), 1):
         if step == 2:
             near = jnp.concatenate([blocks[offset] for offset in (0, -1, 1, -2, 2)], axis=0)
             held += [near, swap(near)]
         if step == 4:
-            far = jnp.concatenate([blocks[offset] for offset in (-3, 3, -4)], axis=0)
+            last = after(blocks[-4], weight_u, weight_v)
+            far = jnp.concatenate([blocks[-3], blocks[3], last], axis=0)
             held += [far, swap(far)]
 
     parts = [None] * 4
@@ -254,15 +241,13 @@
     ).astype(jnp.float32)
     attended = combine(q, suffix_keys, suffix_values, suffix_len.reshape(local, 1), parts)
 
-    late = lax.all_gather(after(out_weight[EARLY:], attended, early), Y, axis=0, tiled=False)
-
-    for step, blocks in enumerate(ring(attended), 1):
-        if step == 3:
-            near = swap(jnp.concatenate([blocks[offset] for offset in (-2, -1, 0, 1, 2)], axis=0))
-    far = swap(jnp.concatenate([blocks[offset] for offset in (3, -4, -3)], axis=0))
-    place = jnp.stack([lax.rem(lax.axis_index("z") + 6, 8), lax.axis_index("c")]).astype(jnp.int32)
-    order = (-2, -1, 0, 1, 2, 3, -4, -3)
-    terms = project(place, [blocks[offset] for offset in order] + [near, far], [early, late])
+    weight_uv = lax.ppermute(weight_u, "v", partner(2, 1))
+
+    own_rows = replicate(attended).reshape(-1, HEADS * HD)
+    place = jnp.stack([lax.axis_index("c"), lax.axis_index(Y)]).astype(jnp.int32)
+    terms = project(
+        place, [own_rows, swap(own_rows)], [out_weight, weight_v, weight_u, weight_uv]
+    )
 
     rows, cols = terms.shape[3:]
     arrived = lax.all_to_all(

time: 197 us -> 191 us (0.970)
  waiting for transfers between devices: 18.8 us -> 49.2 us
  starting transfers between devices: 98.3 us -> 79.8 us
  between operations: 14 us -> 0.5 us
  local copies, waits for them, and re-layouts: 8.64 us -> 4.32 us
    all_to_all x0 -> x1, waiting for transfers between devices: none -> 27.3 us  [replicate(): return lax.all_to_all(sent, 'z', 0, 0, tiled=True)]
    ppermute x4 -> x3, starting transfers between devices: 25.4 us -> 12.7 us  [swap(): return lax.ppermute(value, 'c', partner(2, 1))]
    ppermute x6 -> x3, starting transfers between devices: 30.2 us -> 20.7 us  [ring(): down = lax.ppermute(down, 'z', shift(8, -1))]
    ppermute x8 -> x4, starting transfers between devices: 16.8 us -> 7.67 us  [ring(): up = lax.ppermute(up, 'z', shift(8, 1))]
    ppermute x0 -> x3, starting transfers between devices: none -> 7.3 us  [the longest x1 2.98 us: per_device(): weight_v = lax.ppermute(out_weight, 'v', partner(2, 1))]
    all_to_all x0 -> x1, starting transfers between devices: none -> 6.02 us  [replicate(): return lax.all_to_all(sent, 'z', 0, 0, tiled=True)]
    slice x2 -> x0, local copies, waits for them, and re-layouts: 3.83 us -> none  [the longest x1 2.04 us: per_device(): early = lax.all_gather(out_weight[:EARLY], Y, axis=0, tiled=False)]
    all_to_all x1, waiting for transfers between devices: 1.26 us -> 4.85 us  [per_device(): own = lax.all_to_all(jnp.concatenate(split, axis=1), HEAD, 0, 0, tiled=True)]
  transfers between devices with their start and end apart: 27 -> 21, of which waited for: 8 -> 7; matrix products, arithmetic and copies ran while one was open for 2% -> 1% of each run, Pallas kernels for 6% -> 7%
where the time goes in v3:
time: 191 us; the launch traced here: 190 us
  starting transfers between devices  79.8 us (42%)
  waiting for transfers between devices  49.2 us (26%)
  blocking collectives  35.8 us (19%)
  Pallas kernels  18.4 us (10%)
  local copies, waits for them, and re-layouts  4.32 us (2%)
    all_to_all x1, blocking collectives, per_device(): lax.all_to_all(terms.reshape(32, 2 * rows, cols), Y + HEAD, 0, 0, tiled=T...  35.8 us
    all_to_all x1, waiting for transfers between devices, replicate(): return lax.all_to_all(sent, 'z', 0, 0, tiled=True)  27.3 us
    ppermute x3, starting transfers between devices, ring(): down = lax.ppermute(down, 'z', shift(8, -1))  20.7 us
    pallas_call x4, Pallas kernels, attend(): pl.pallas_call(attention_kernel, out_shape=jax.ShapeDtypeStruct((rows, HE...  13.1 us
    ppermute x3, starting transfers between devices, swap(): return lax.ppermute(value, 'c', partner(2, 1))  12.7 us
    ppermute x4, waiting for transfers between devices, ring(): up = lax.ppermute(up, 'z', shift(8, 1))  10.9 us
    ppermute x3, starting transfers between devices, per_device(): parts[k] = message if k == 0 else lax.ppermute(message, Y, partner(4, k))  8.55 us
    all_to_all x1, starting transfers between devices, per_device(): own = lax.all_to_all(jnp.concatenate(split, axis=1), HEAD, 0, 0, tiled=True)  8.51 us
  transfers between devices with their start and end apart: 21, of which 7 were waited for; matrix products, arithmetic and copies ran while one was open for 1% of the time, Pallas kernels for 7%

profile of v3, /device:TPU:9, one launch (start us, length us, event | category | flops | bytes accessed | tf_op | source)
XLA Modules:
  0.0 189.9 jit_solution(2443748048327637425)
XLA Ops:
  0.0 0.8 copy-done
  0.8 0.9 bitcast_bitcast_fusion
  1.7 0.7 pad_maximum_fusion.1
  2.4 8.5 %all-to-all-start = ((bf16[8,64,128]{2,1,0:T(8,128)(2,1)}), bf16[8,64,128]{2,1,0:T(8,128)(2,1)S(1)}, u32[]{:S(2)}, u32[]{:S(2)}) async-start(bf16[8,64,128]{2,1,0:T(8,128)(2,1)} %pad_maximum_fusion.1), calls=%async_computation | async-start | bytes 262144 | tf_op jit(solution)/shard_map/all_to_all | solution.py:218
  10.9 2.4 %collective-permute-start.8 = (bf16[2048,256]{1,0:T(8,128)(2,1)}, bf16[2048,256]{1,0:T(8,128)(2,1)}, u32[]{:S(2)}, u32[]{:S(2)}) collective-permute-start(bf16[2048,256]{1,0:T(8,128)(2,1)} %refs_0_.1), channel_id=1, source_target_pairs={{0,32},{32,0},{1,33},{33,1},{2,34},{34,2},{3,35},{35,3},{4,36},{36... | collective-permute-start | bytes 3145736 | tf_op jit(solution)/shard_map/ppermute | solution.py:219
  13.3 3.0 %collective-permute-start.9 = (bf16[2048,256]{1,0:T(8,128)(2,1)}, bf16[2048,256]{1,0:T(8,128)(2,1)S(1)}, u32[]{:S(2)}, u32[]{:S(2)}) collective-permute-start(bf16[2048,256]{1,0:T(8,128)(2,1)} %refs_0_.1), channel_id=1, source_target_pairs={{0,16},{16,0},{1,17},{17,1},{2,18},{18,2},{3,19},{19,3},{4,20},{20... | collective-permute-start | bytes 3145736 | tf_op jit(solution)/shard_map/ppermute | solution.py:220
  16.3 4.9 %all-to-all-done = bf16[8,64,128]{2,1,0:T(8,128)(2,1)S(1)} async-done(((bf16[8,64,128]{2,1,0:T(8,128)(2,1)}), bf16[8,64,128]{2,1,0:T(8,128)(2,1)S(1)}, u32[]{:S(2)}, u32[]{:S(2)}) %all-to-all-start) | async-done | bytes 131104 | tf_op jit(solution)/shard_map/all_to_all | solution.py:218
  21.1 10.7 %collective-permute-start.1 = (bf16[8,64,128]{2,1,0:T(8,128)(2,1)S(1)}, bf16[8,64,128]{2,1,0:T(8,128)(2,1)S(1)}, u32[]{:S(2)}, u32[]{:S(2)}) collective-permute-start(bf16[8,64,128]{2,1,0:T(8,128)(2,1)S(1)} %all-to-all-done), channel_id=1, source_target_pairs={{0,448},{64,0},{128,64},{192,128},{256,192},{320,256},{384,320},{4... | collective-permute-start | bytes 393224 | tf_op jit(solution)/shard_map/ppermute | solution.py:39
  31.8 1.9 %collective-permute-start = (bf16[8,64,128]{2,1,0:T(8,128)(2,1)S(1)}, bf16[8,64,128]{2,1,0:T(8,128)(2,1)S(1)}, u32[]{:S(2)}, u32[]{:S(2)}) collective-permute-start(bf16[8,64,128]{2,1,0:T(8,128)(2,1)S(1)} %all-to-all-done), channel_id=1, source_target_pairs={{0,64},{64,128},{128,192},{192,256},{256,320},{320,384},{384,448},... | collective-permute-start | bytes 393224 | tf_op jit(solution)/shard_map/ppermute | solution.py:36
  33.8 0.0 collective-permute-done.1
  33.8 5.2 %collective-permute-start.3 = (bf16[8,64,128]{2,1,0:T(8,128)(2,1)S(1)}, bf16[8,64,128]{2,1,0:T(8,128)(2,1)S(1)}, u32[]{:S(2)}, u32[]{:S(2)}) collective-permute-start(bf16[8,64,128]{2,1,0:T(8,128)(2,1)S(1)} %collective-permute-done.1), channel_id=1, source_target_pairs={{0,448},{64,0},{128,64},{192,128},{256,192},{320,256},{384,320},{4... | collective-permute-start | bytes 393224 | tf_op jit(solution)/shard_map/ppermute | solution.py:39
  39.0 0.0 collective-permute-done
  39.0 1.9 %collective-permute-start.2 = (bf16[8,64,128]{2,1,0:T(8,128)(2,1)S(1)}, bf16[8,64,128]{2,1,0:T(8,128)(2,1)S(1)}, u32[]{:S(2)}, u32[]{:S(2)}) collective-permute-start(bf16[8,64,128]{2,1,0:T(8,128)(2,1)S(1)} %collective-permute-done), channel_id=1, source_target_pairs={{0,64},{64,128},{128,192},{192,256},{256,320},{320,384},{384,448},... | collective-permute-start | bytes 393224 | tf_op jit(solution)/shard_map/ppermute | solution.py:36
  41.0 4.9 %collective-permute-done.2 = bf16[8,64,128]{2,1,0:T(8,128)(2,1)S(1)} collective-permute-done((bf16[8,64,128]{2,1,0:T(8,128)(2,1)S(1)}, bf16[8,64,128]{2,1,0:T(8,128)(2,1)S(1)}, u32[]{:S(2)}, u32[]{:S(2)}) %collective-permute-start.2) | collective-permute-done | bytes 131104 | tf_op jit(solution)/shard_map/ppermute | solution.py:36
  45.9 1.9 %collective-permute-start.5 = (bf16[8,64,128]{2,1,0:T(8,128)(2,1)S(1)}, bf16[8,64,128]{2,1,0:T(8,128)(2,1)S(1)}, u32[]{:S(2)}, u32[]{:S(2)}) collective-permute-start(bf16[8,64,128]{2,1,0:T(8,128)(2,1)S(1)} %collective-permute-done.2), channel_id=1, source_target_pairs={{0,64},{64,128},{128,192},{192,256},{256,320},{320,384},{384,448},... | collective-permute-start | bytes 393224 | tf_op jit(solution)/shard_map/ppermute | solution.py:36
  47.8 0.0 copy-start.4
  47.9 0.0 collective-permute-done.3
  47.9 0.0 copy-start.7
  47.9 6.5 %collective-permute-start.4 = (bf16[40,64,128]{2,1,0:T(8,128)(2,1)S(1)}, bf16[40,64,128]{2,1,0:T(8,128)(2,1)S(1)}, u32[]{:S(2)}, u32[]{:S(2)}) collective-permute-start(bf16[40,64,128]{2,1,0:T(8,128)(2,1)S(1)} %constant_dynamic-update-slice_fusion.refs_0_), channel_id=1, source_target_pairs={{0,8},{8,0},{1,9},{9,1},{2,10},{10,2},{3,11},{11,3},{4,12},{12,4},... | collective-permute-start | bytes 1966088 | tf_op jit(solution)/shard_map/ppermute | solution.py:50
  54.4 4.9 %collective-permute-start.6 = (bf16[8,64,128]{2,1,0:T(8,128)(2,1)S(1)}, bf16[8,64,128]{2,1,0:T(8,128)(2,1)S(1)}, u32[]{:S(2)}, u32[]{:S(2)}) collective-permute-start(bf16[8,64,128]{2,1,0:T(8,128)(2,1)S(1)} %collective-permute-done.3), channel_id=1, source_target_pairs={{0,448},{64,0},{128,64},{192,128},{256,192},{320,256},{384,320},{4... | collective-permute-start | bytes 393224 | tf_op jit(solution)/shard_map/ppermute | solution.py:39
  59.3 0.0 collective-permute-done.5
  59.3 1.9 %collective-permute-start.7 = (bf16[8,64,128]{2,1,0:T(8,128)(2,1)S(1)}, bf16[8,64,128]{2,1,0:T(8,128)(2,1)S(1)}, u32[]{:S(2)}, u32[]{:S(2)}) collective-permute-start(bf16[8,64,128]{2,1,0:T(8,128)(2,1)S(1)} %collective-permute-done.5), channel_id=1, source_target_pairs={{0,64},{64,128},{128,192},{192,256},{256,320},{320,384},{384,448},... | collective-permute-start | bytes 393224 | tf_op jit(solution)/shard_map/ppermute | solution.py:36
  61.2 5.9 %collective-permute-done.7.refs_0_ = bf16[8,64,128]{2,1,0:T(8,128)(2,1)S(1)} collective-permute-done((bf16[8,64,128]{2,1,0:T(8,128)(2,1)S(1)}, bf16[8,64,128]{2,1,0:T(8,128)(2,1)S(1)}, u32[]{:S(2)}, u32[]{:S(2)}) %collective-permute-start.7) | collective-permute-done | bytes 131104 | tf_op jit(solution)/shard_map/ppermute | solution.py:36
  67.2 2.3 %collective-permute-start.15 = (bf16[32,2048]{1,0:T(8,128)(2,1)S(1)}, bf16[32,2048]{1,0:T(8,128)(2,1)S(1)}, u32[]{:S(2)}, u32[]{:S(2)}) collective-permute-start(bf16[32,2048]{1,0:T(8,128)(2,1)S(1)} %bitcast.34), channel_id=1, source_target_pairs={{0,48},{16,32},{32,16},{48,0},{1,49},{17,33},{33,17},{49,1},{2,50}... | collective-permute-start | bytes 393224 | tf_op jit(solution)/shard_map/ppermute | solution.py:213
  69.4 0.0 collective-permute-done.8.refs_1_.refs_2_
  69.5 3.9 %collective-permute-start.13 = (bf16[32,2048]{1,0:T(8,128)(2,1)S(1)}, bf16[32,2048]{1,0:T(8,128)(2,1)}, u32[]{:S(2)}, u32[]{:S(2)}) collective-permute-start(bf16[32,2048]{1,0:T(8,128)(2,1)S(1)} %bitcast.35), channel_id=1, source_target_pairs={{0,32},{16,48},{32,0},{48,16},{1,33},{17,49},{33,1},{49,17},{2,34}... | collective-permute-start | bytes 393224 | tf_op jit(solution)/shard_map/ppermute | solution.py:213
  73.4 0.0 collective-permute-done.9.refs_2_.refs_1_
  73.4 2.2 %collective-permute-start.11 = (bf16[32,2048]{1,0:T(8,128)(2,1)S(1)}, bf16[32,2048]{1,0:T(8,128)(2,1)}, u32[]{:S(2)}, u32[]{:S(2)}) collective-permute-start(bf16[32,2048]{1,0:T(8,128)(2,1)S(1)} %bitcast.36), channel_id=1, source_target_pairs={{0,16},{16,0},{32,48},{48,32},{1,17},{17,1},{33,49},{49,33},{2,18}... | collective-permute-start | bytes 393224 | tf_op jit(solution)/shard_map/ppermute | solution.py:213
  75.6 0.0 collective-permute-done.6
  75.6 1.0 pad_maximum_fusion.refs_2_
  76.6 3.9 %collective-permute-start.10 = (bf16[24,64,128]{2,1,0:T(8,128)(2,1)S(1)}, bf16[24,64,128]{2,1,0:T(8,128)(2,1)S(1)}, u32[]{:S(2)}, u32[]{:S(2)}) collective-permute-start(bf16[24,64,128]{2,1,0:T(8,128)(2,1)S(1)} %pad_maximum_fusion.refs_2_), channel_id=1, source_target_pairs={{0,8},{8,0},{1,9},{9,1},{2,10},{10,2},{3,11},{11,3},{4,12},{12,4},... | collective-permute-start | bytes 1179656 | tf_op jit(solution)/shard_map/ppermute | solution.py:50
  80.5 0.0 collective-permute-done.11.q_ref
  80.5 0.0 collective-permute-done.4.refs_1_
  80.5 1.3 collective-permute-done.10.refs_3_
  81.8 3.7 %attend.5 = bf16[32,2176]{1,0:T(8,128)(2,1)S(1)} custom-call(bf16[32,2048]{1,0:T(8,128)(2,1)} %collective-permute-done.11.q_ref, bf16[40,64,128]{2,1,0:T(8,128)(2,1)S(1)} %constant_dynamic-update-slice_fusion.refs_0_, bf16[40,64,128]{2,1,0:T(8,128)(2,1)S(1)} %collective-permute-done.4.refs_1_, bf16[24,64,128]{2,1,0:T(8,128)(2,1)S(1)} %pad_maximum_fusion.refs_2_, ...), custom_call_target="tpu_custom_call" | custom-call | tf_op jit(solution)/shard_map/attend/pallas_call | solution.py:109
  85.5 3.1 %collective-permute-start.12 = (bf16[32,2176]{1,0:T(8,128)(2,1)S(1)}, bf16[32,2176]{1,0:T(8,128)(2,1)S(1)}, u32[]{:S(2)}, u32[]{:S(2)}) collective-permute-start(bf16[32,2176]{1,0:T(8,128)(2,1)S(1)} %attend.5), channel_id=1, source_target_pairs={{0,16},{16,0},{32,48},{48,32},{1,17},{17,1},{33,49},{49,33},{2,18}... | collective-permute-start | bytes 417800 | tf_op jit(solution)/shard_map/ppermute | solution.py:234
  88.6 0.0 collective-permute-done.13.q_ref
  88.6 3.7 %attend.6 = bf16[32,2176]{1,0:T(8,128)(2,1)S(1)} custom-call(bf16[32,2048]{1,0:T(8,128)(2,1)} %collective-permute-done.13.q_ref, bf16[40,64,128]{2,1,0:T(8,128)(2,1)S(1)} %constant_dynamic-update-slice_fusion.refs_0_, bf16[40,64,128]{2,1,0:T(8,128)(2,1)S(1)} %collective-permute-done.4.refs_1_, bf16[24,64,128]{2,1,0:T(8,128)(2,1)S(1)} %pad_maximum_fusion.refs_2_, ...), custom_call_target="tpu_custom_call" | custom-call | tf_op jit(solution)/shard_map/attend/pallas_call | solution.py:109
  92.3 2.3 %collective-permute-start.14 = (bf16[32,2176]{1,0:T(8,128)(2,1)S(1)}, bf16[32,2176]{1,0:T(8,128)(2,1)S(1)}, u32[]{:S(2)}, u32[]{:S(2)}) collective-permute-start(bf16[32,2176]{1,0:T(8,128)(2,1)S(1)} %attend.6), channel_id=1, source_target_pairs={{0,32},{16,48},{32,0},{48,16},{1,33},{17,49},{33,1},{49,17},{2,34}... | collective-permute-start | bytes 417800 | tf_op jit(solution)/shard_map/ppermute | solution.py:234
  94.6 0.0 collective-permute-done.15.q_ref
  94.7 0.0 copy-start.8
  94.7 0.0 copy-start.10
  94.7 2.8 %attend.7 = bf16[32,2176]{1,0:T(8,128)(2,1)S(1)} custom-call(bf16[32,2048]{1,0:T(8,128)(2,1)S(1)} %collective-permute-done.15.q_ref, bf16[40,64,128]{2,1,0:T(8,128)(2,1)S(1)} %constant_dynamic-update-slice_fusion.refs_0_, bf16[40,64,128]{2,1,0:T(8,128)(2,1)S(1)} %collective-permute-done.4.refs_1_, bf16[24,64,128]{2,1,0:T(8,128)(2,1)S(1)} %pad_maximum_fusion.refs_2_, ...), custom_call_target="tpu_custom_call" | custom-call | tf_op jit(solution)/shard_map/attend/pallas_call | solution.py:109
  97.5 3.2 %collective-permute-start.16 = (bf16[32,2176]{1,0:T(8,128)(2,1)S(1)}, bf16[32,2176]{1,0:T(8,128)(2,1)S(1)}, u32[]{:S(2)}, u32[]{:S(2)}) collective-permute-start(bf16[32,2176]{1,0:T(8,128)(2,1)S(1)} %attend.7), channel_id=1, source_target_pairs={{0,48},{16,32},{32,16},{48,0},{1,49},{17,33},{33,17},{49,1},{2,50}... | collective-permute-start | bytes 417800 | tf_op jit(solution)/shard_map/ppermute | solution.py:234
  100.7 0.0 copy-start.9
  100.8 0.1 copy.36.len_ref
  100.8 0.6 copy-done.9
  101.4 2.8 %attend.4.m0_ref = bf16[32,2176]{1,0:T(8,128)(2,1)S(1)} custom-call(bf16[32,2048]{1,0:T(8,128)(2,1)S(1)} %bitcast.37, bf16[40,64,128]{2,1,0:T(8,128)(2,1)S(1)} %constant_dynamic-update-slice_fusion.refs_0_, bf16[40,64,128]{2,1,0:T(8,128)(2,1)S(1)} %collective-permute-done.4.refs_1_, bf16[24,64,128]{2,1,0:T(8,128)(2,1)S(1)} %pad_maximum_fusion.refs_2_, ...), custom_call_target="tpu_custom_call" | custom-call | tf_op jit(solution)/shard_map/attend/pallas_call | solution.py:109
  104.3 0.0 collective-permute-done.12.m1_ref
  104.3 0.0 collective-permute-done.14.m2_ref
  104.3 2.5 %collective-permute-done.16.m3_ref = bf16[32,2176]{1,0:T(8,128)(2,1)S(1)} collective-permute-done((bf16[32,2176]{1,0:T(8,128)(2,1)S(1)}, bf16[32,2176]{1,0:T(8,128)(2,1)S(1)}, u32[]{:S(2)}, u32[]{:S(2)}) %collective-permute-start.16) | collective-permute-done | bytes 139296 | tf_op jit(solution)/shard_map/ppermute | solution.py:234
  106.8 1.0 combine.1
  107.9 1.1 broadcast_in_dim.2
  109.0 6.0 %all-to-all-start.1 = ((bf16[8,32,2048]{2,1,0:T(8,128)(2,1)}), bf16[8,32,2048]{2,1,0:T(8,128)(2,1)S(1)}, u32[]{:S(2)}, u32[]{:S(2)}) async-start(bf16[8,32,2048]{2,1,0:T(8,128)(2,1)} %broadcast_in_dim.2), calls=%async_computation.1 | async-start | bytes 2097152 | tf_op jit(solution)/shard_map/all_to_all | solution.py:46
  115.0 1.9 %collective-permute-start.18 = (bf16[2048,256]{1,0:T(8,128)(2,1)}, bf16[2048,256]{1,0:T(8,128)(2,1)}, u32[]{:S(2)}, u32[]{:S(2)}) collective-permute-start(bf16[2048,256]{1,0:T(8,128)(2,1)} %collective-permute-done.8.refs_1_.refs_2_), channel_id=1, source_target_pairs={{0,16},{16,0},{1,17},{17,1},{2,18},{18,2},{3,19},{19,3},{4,20},{20... | collective-permute-start | bytes 3145736 | tf_op jit(solution)/shard_map/ppermute | solution.py:244
  116.9 27.3 %all-to-all-done.1 = bf16[8,32,2048]{2,1,0:T(8,128)(2,1)S(1)} async-done(((bf16[8,32,2048]{2,1,0:T(8,128)(2,1)}), bf16[8,32,2048]{2,1,0:T(8,128)(2,1)S(1)}, u32[]{:S(2)}, u32[]{:S(2)}) %all-to-all-start.1) | async-done | bytes 1048608 | tf_op jit(solution)/shard_map/all_to_all | solution.py:46
  144.2 2.4 %collective-permute-start.17 = (bf16[256,2048]{1,0:T(8,128)(2,1)S(1)}, bf16[256,2048]{1,0:T(8,128)(2,1)}, u32[]{:S(2)}, u32[]{:S(2)}) collective-permute-start(bf16[256,2048]{1,0:T(8,128)(2,1)S(1)} %bitcast.31), channel_id=1, source_target_pairs={{0,8},{8,0},{1,9},{9,1},{2,10},{10,2},{3,11},{11,3},{4,12},{12,4},... | collective-permute-start | bytes 3145736 | tf_op jit(solution)/shard_map/ppermute | solution.py:50
  146.6 0.1 pad_add_fusion.place_ref
  146.6 0.0 collective-permute-done.18.refs_3_
  146.7 2.3 %collective-permute-done.17.other_ref = bf16[256,2048]{1,0:T(8,128)(2,1)} collective-permute-done((bf16[256,2048]{1,0:T(8,128)(2,1)S(1)}, bf16[256,2048]{1,0:T(8,128)(2,1)}, u32[]{:S(2)}, u32[]{:S(2)}) %collective-permute-start.17) | collective-permute-done | bytes 1048608 | tf_op jit(solution)/shard_map/ppermute | solution.py:50
  149.0 4.2 %project.1 = bf16[4,8,2,32,256]{4,3,2,1,0:T(8,128)(2,1)S(1)} custom-call(s32[2]{0:T(128)S(1)} %pad_add_fusion.place_ref, bf16[256,2048]{1,0:T(8,128)(2,1)S(1)} %bitcast.32, bf16[256,2048]{1,0:T(8,128)(2,1)} %collective-permute-done.17.other_ref, bf16[2048,256]{1,0:T(8,128)(2,1)S(1)} %copy-done.3, bf16[2048,256]{1,0:T(8,128)(2,1)S(1)} %copy-done.2, ...), custom_call_target="tpu_custom_call" | custom-call | tf_op jit(solution)/shard_map/project/pallas_call | solution.py:188
  153.2 35.8 %all_to_all.15 = bf16[32,64,256]{2,1,0:T(8,128)(2,1)S(1)} all-to-all(bf16[32,64,256]{2,1,0:T(8,128)(2,1)S(1)} %bitcast.33), channel_id=1, replica_groups=mesh['z'=8,'u'=2,'v'=2,'c'=2,'x'=4,'w'=2] {'u','v','x','w'}, dimensions={0} | all-to-all | bytes 2097152 | tf_op jit(solution)/shard_map/all_to_all | solution.py:253
  189.0 0.2 reduce_sum.12
  189.2 0.7 copy.37
  (27 shorter events, 0.2 us)
Async XLA Ops:
  0.0 0.8 copy-start
  2.4 31.4 %copy-start.6 = (bf16[16,2,128]{2,1,0:T(2,128)(2,1)S(1)}, bf16[16,2,128]{2,1,0:T(2,128)(2,1)}, u32[]{:S(2)}) copy-start(bf16[16,2,128]{2,1,0:T(2,128)(2,1)} %param.12) | copy-start | bytes 24580
  2.4 18.8 %all-to-all-start = ((bf16[8,64,128]{2,1,0:T(8,128)(2,1)}), bf16[8,64,128]{2,1,0:T(8,128)(2,1)S(1)}, u32[]{:S(2)}, u32[]{:S(2)}) async-start(bf16[8,64,128]{2,1,0:T(8,128)(2,1)} %pad_maximum_fusion.1), calls=%async_computation | async-start | bytes 262144 | tf_op jit(solution)/shard_map/all_to_all | solution.py:218
  10.9 58.6 %collective-permute-start.8 = (bf16[2048,256]{1,0:T(8,128)(2,1)}, bf16[2048,256]{1,0:T(8,128)(2,1)}, u32[]{:S(2)}, u32[]{:S(2)}) collective-permute-start(bf16[2048,256]{1,0:T(8,128)(2,1)} %refs_0_.1), channel_id=1, source_target_pairs={{0,32},{32,0},{1,33},{33,1},{2,34},{34,2},{3,35},{35,3},{4,36},{36... | collective-permute-start | bytes 3145736 | tf_op jit(solution)/shard_map/ppermute | solution.py:219
  13.3 60.1 %collective-permute-start.9 = (bf16[2048,256]{1,0:T(8,128)(2,1)}, bf16[2048,256]{1,0:T(8,128)(2,1)S(1)}, u32[]{:S(2)}, u32[]{:S(2)}) collective-permute-start(bf16[2048,256]{1,0:T(8,128)(2,1)} %refs_0_.1), channel_id=1, source_target_pairs={{0,16},{16,0},{1,17},{17,1},{2,18},{18,2},{3,19},{19,3},{4,20},{20... | collective-permute-start | bytes 3145736 | tf_op jit(solution)/shard_map/ppermute | solution.py:220
  21.1 12.6 %collective-permute-start.1 = (bf16[8,64,128]{2,1,0:T(8,128)(2,1)S(1)}, bf16[8,64,128]{2,1,0:T(8,128)(2,1)S(1)}, u32[]{:S(2)}, u32[]{:S(2)}) collective-permute-start(bf16[8,64,128]{2,1,0:T(8,128)(2,1)S(1)} %all-to-all-done), channel_id=1, source_target_pairs={{0,448},{64,0},{128,64},{192,128},{256,192},{320,256},{384,320},{4... | collective-permute-start | bytes 393224 | tf_op jit(solution)/shard_map/ppermute | solution.py:39
  31.8 7.2 %collective-permute-start = (bf16[8,64,128]{2,1,0:T(8,128)(2,1)S(1)}, bf16[8,64,128]{2,1,0:T(8,128)(2,1)S(1)}, u32[]{:S(2)}, u32[]{:S(2)}) collective-permute-start(bf16[8,64,128]{2,1,0:T(8,128)(2,1)S(1)} %all-to-all-done), channel_id=1, source_target_pairs={{0,64},{64,128},{128,192},{192,256},{256,320},{320,384},{384,448},... | collective-permute-start | bytes 393224 | tf_op jit(solution)/shard_map/ppermute | solution.py:36
  33.8 14.1 %collective-permute-start.3 = (bf16[8,64,128]{2,1,0:T(8,128)(2,1)S(1)}, bf16[8,64,128]{2,1,0:T(8,128)(2,1)S(1)}, u32[]{:S(2)}, u32[]{:S(2)}) collective-permute-start(bf16[8,64,128]{2,1,0:T(8,128)(2,1)S(1)} %collective-permute-done.1), channel_id=1, source_target_pairs={{0,448},{64,0},{128,64},{192,128},{256,192},{320,256},{384,320},{4... | collective-permute-start | bytes 393224 | tf_op jit(solution)/shard_map/ppermute | solution.py:39
  39.0 6.9 %collective-permute-start.2 = (bf16[8,64,128]{2,1,0:T(8,128)(2,1)S(1)}, bf16[8,64,128]{2,1,0:T(8,128)(2,1)S(1)}, u32[]{:S(2)}, u32[]{:S(2)}) collective-permute-start(bf16[8,64,128]{2,1,0:T(8,128)(2,1)S(1)} %collective-permute-done), channel_id=1, source_target_pairs={{0,64},{64,128},{128,192},{192,256},{256,320},{320,384},{384,448},... | collective-permute-start | bytes 393224 | tf_op jit(solution)/shard_map/ppermute | solution.py:36
  45.9 13.4 %collective-permute-start.5 = (bf16[8,64,128]{2,1,0:T(8,128)(2,1)S(1)}, bf16[8,64,128]{2,1,0:T(8,128)(2,1)S(1)}, u32[]{:S(2)}, u32[]{:S(2)}) collective-permute-start(bf16[8,64,128]{2,1,0:T(8,128)(2,1)S(1)} %collective-permute-done.2), channel_id=1, source_target_pairs={{0,64},{64,128},{128,192},{192,256},{256,320},{320,384},{384,448},... | collective-permute-start | bytes 393224 | tf_op jit(solution)/shard_map/ppermute | solution.py:36
  47.8 19.3 %copy-start.4 = (bf16[2,16,2048]{2,1,0:T(8,128)(2,1)S(1)}, bf16[2,16,2048]{2,1,0:T(8,128)(2,1)}, u32[]{:S(2)}) copy-start(bf16[2,16,2048]{2,1,0:T(8,128)(2,1)} %param.9) | copy-start | bytes 393220
  47.9 13.3 %copy-start.7 = (bf16[16,2,128]{2,1,0:T(2,128)(2,1)S(1)}, bf16[16,2,128]{2,1,0:T(2,128)(2,1)}, u32[]{:S(2)}) copy-start(bf16[16,2,128]{2,1,0:T(2,128)(2,1)} %param.13) | copy-start | bytes 24580
  47.9 32.6 %collective-permute-start.4 = (bf16[40,64,128]{2,1,0:T(8,128)(2,1)S(1)}, bf16[40,64,128]{2,1,0:T(8,128)(2,1)S(1)}, u32[]{:S(2)}, u32[]{:S(2)}) collective-permute-start(bf16[40,64,128]{2,1,0:T(8,128)(2,1)S(1)} %constant_dynamic-update-slice_fusion.refs_0_), channel_id=1, source_target_pairs={{0,8},{8,0},{1,9},{9,1},{2,10},{10,2},{3,11},{11,3},{4,12},{12,4},... | collective-permute-start | bytes 1966088 | tf_op jit(solution)/shard_map/ppermute | solution.py:50
  54.4 21.2 %collective-permute-start.6 = (bf16[8,64,128]{2,1,0:T(8,128)(2,1)S(1)}, bf16[8,64,128]{2,1,0:T(8,128)(2,1)S(1)}, u32[]{:S(2)}, u32[]{:S(2)}) collective-permute-start(bf16[8,64,128]{2,1,0:T(8,128)(2,1)S(1)} %collective-permute-done.3), channel_id=1, source_target_pairs={{0,448},{64,0},{128,64},{192,128},{256,192},{320,256},{384,320},{4... | collective-permute-start | bytes 393224 | tf_op jit(solution)/shard_map/ppermute | solution.py:39
  59.3 7.9 %collective-permute-start.7 = (bf16[8,64,128]{2,1,0:T(8,128)(2,1)S(1)}, bf16[8,64,128]{2,1,0:T(8,128)(2,1)S(1)}, u32[]{:S(2)}, u32[]{:S(2)}) collective-permute-start(bf16[8,64,128]{2,1,0:T(8,128)(2,1)S(1)} %collective-permute-done.5), channel_id=1, source_target_pairs={{0,64},{64,128},{128,192},{192,256},{256,320},{320,384},{384,448},... | collective-permute-start | bytes 393224 | tf_op jit(solution)/shard_map/ppermute | solution.py:36
  67.2 8.4 %copy-start.5 = (bf16[8,64,128]{2,1,0:T(8,128)(2,1)}, bf16[8,64,128]{2,1,0:T(8,128)(2,1)S(1)}, u32[]{:S(2)}) copy-start(bf16[8,64,128]{2,1,0:T(8,128)(2,1)S(1)} %collective-permute-done.7.refs_0_) | copy-start | bytes 393220
  67.2 27.5 %collective-permute-start.15 = (bf16[32,2048]{1,0:T(8,128)(2,1)S(1)}, bf16[32,2048]{1,0:T(8,128)(2,1)S(1)}, u32[]{:S(2)}, u32[]{:S(2)}) collective-permute-start(bf16[32,2048]{1,0:T(8,128)(2,1)S(1)} %bitcast.34), channel_id=1, source_target_pairs={{0,48},{16,32},{32,16},{48,0},{1,49},{17,33},{33,17},{49,1},{2,50}... | collective-permute-start | bytes 393224 | tf_op jit(solution)/shard_map/ppermute | solution.py:213
  69.5 19.2 %collective-permute-start.13 = (bf16[32,2048]{1,0:T(8,128)(2,1)S(1)}, bf16[32,2048]{1,0:T(8,128)(2,1)}, u32[]{:S(2)}, u32[]{:S(2)}) collective-permute-start(bf16[32,2048]{1,0:T(8,128)(2,1)S(1)} %bitcast.35), channel_id=1, source_target_pairs={{0,32},{16,48},{32,0},{48,16},{1,33},{17,49},{33,1},{49,17},{2,34}... | collective-permute-start | bytes 393224 | tf_op jit(solution)/shard_map/ppermute | solution.py:213
  73.4 2.2 %copy-start.1 = (bf16[2048,256]{1,0:T(8,128)(2,1)}, bf16[2048,256]{1,0:T(8,128)(2,1)S(1)}, u32[]{:S(2)}) copy-start(bf16[2048,256]{1,0:T(8,128)(2,1)S(1)} %collective-permute-done.9.refs_2_.refs_1_) | copy-start | bytes 3145732
  73.4 7.1 %collective-permute-start.11 = (bf16[32,2048]{1,0:T(8,128)(2,1)S(1)}, bf16[32,2048]{1,0:T(8,128)(2,1)}, u32[]{:S(2)}, u32[]{:S(2)}) collective-permute-start(bf16[32,2048]{1,0:T(8,128)(2,1)S(1)} %bitcast.36), channel_id=1, source_target_pairs={{0,16},{16,0},{32,48},{48,32},{1,17},{17,1},{33,49},{49,33},{2,18}... | collective-permute-start | bytes 393224 | tf_op jit(solution)/shard_map/ppermute | solution.py:213
  76.6 5.2 %collective-permute-start.10 = (bf16[24,64,128]{2,1,0:T(8,128)(2,1)S(1)}, bf16[24,64,128]{2,1,0:T(8,128)(2,1)S(1)}, u32[]{:S(2)}, u32[]{:S(2)}) collective-permute-start(bf16[24,64,128]{2,1,0:T(8,128)(2,1)S(1)} %pad_maximum_fusion.refs_2_), channel_id=1, source_target_pairs={{0,8},{8,0},{1,9},{9,1},{2,10},{10,2},{3,11},{11,3},{4,12},{12,4},... | collective-permute-start | bytes 1179656 | tf_op jit(solution)/shard_map/ppermute | solution.py:50
  85.5 18.8 %collective-permute-start.12 = (bf16[32,2176]{1,0:T(8,128)(2,1)S(1)}, bf16[32,2176]{1,0:T(8,128)(2,1)S(1)}, u32[]{:S(2)}, u32[]{:S(2)}) collective-permute-start(bf16[32,2176]{1,0:T(8,128)(2,1)S(1)} %attend.5), channel_id=1, source_target_pairs={{0,16},{16,0},{32,48},{48,32},{1,17},{17,1},{33,49},{49,33},{2,18}... | collective-permute-start | bytes 417800 | tf_op jit(solution)/shard_map/ppermute | solution.py:234
  92.3 11.9 %collective-permute-start.14 = (bf16[32,2176]{1,0:T(8,128)(2,1)S(1)}, bf16[32,2176]{1,0:T(8,128)(2,1)S(1)}, u32[]{:S(2)}, u32[]{:S(2)}) collective-permute-start(bf16[32,2176]{1,0:T(8,128)(2,1)S(1)} %attend.6), channel_id=1, source_target_pairs={{0,32},{16,48},{32,0},{48,16},{1,33},{17,49},{33,1},{49,17},{2,34}... | collective-permute-start | bytes 417800 | tf_op jit(solution)/shard_map/ppermute | solution.py:234
  94.7 6.1 %copy-start.8 = (bf16[2,16,128]{2,1,0:T(8,128)(2,1)S(1)}, bf16[2,16,128]{2,1,0:T(8,128)(2,1)}, u32[]{:S(2)}) copy-start(bf16[2,16,128]{2,1,0:T(8,128)(2,1)} %param.15) | copy-start | bytes 24580
  94.7 6.1 %copy-start.10 = (s32[16]{0:T(128)S(1)}, s32[16]{0:T(128)}, u32[]{:S(2)}) copy-start(s32[16]{0:T(128)} %param.16) | copy-start | bytes 196
  97.5 9.3 %collective-permute-start.16 = (bf16[32,2176]{1,0:T(8,128)(2,1)S(1)}, bf16[32,2176]{1,0:T(8,128)(2,1)S(1)}, u32[]{:S(2)}, u32[]{:S(2)}) collective-permute-start(bf16[32,2176]{1,0:T(8,128)(2,1)S(1)} %attend.7), channel_id=1, source_target_pairs={{0,48},{16,32},{32,16},{48,0},{1,49},{17,33},{33,17},{49,1},{2,50}... | collective-permute-start | bytes 417800 | tf_op jit(solution)/shard_map/ppermute | solution.py:234
  100.7 0.7 copy-start.9
  109.0 40.0 %copy-start.2 = (bf16[2048,256]{1,0:T(8,128)(2,1)S(1)}, bf16[2048,256]{1,0:T(8,128)(2,1)}, u32[]{:S(2)}) copy-start(bf16[2048,256]{1,0:T(8,128)(2,1)} %copy-done.1) | copy-start | bytes 3145732
  109.0 40.0 %copy-start.3 = (bf16[2048,256]{1,0:T(8,128)(2,1)S(1)}, bf16[2048,256]{1,0:T(8,128)(2,1)}, u32[]{:S(2)}) copy-start(bf16[2048,256]{1,0:T(8,128)(2,1)} %refs_0_.1) | copy-start | bytes 3145732
  109.0 35.2 %all-to-all-start.1 = ((bf16[8,32,2048]{2,1,0:T(8,128)(2,1)}), bf16[8,32,2048]{2,1,0:T(8,128)(2,1)S(1)}, u32[]{:S(2)}, u32[]{:S(2)}) async-start(bf16[8,32,2048]{2,1,0:T(8,128)(2,1)} %broadcast_in_dim.2), calls=%async_computation.1 | async-start | bytes 2097152 | tf_op jit(solution)/shard_map/all_to_all | solution.py:46
  115.0 31.7 %collective-permute-start.18 = (bf16[2048,256]{1,0:T(8,128)(2,1)}, bf16[2048,256]{1,0:T(8,128)(2,1)}, u32[]{:S(2)}, u32[]{:S(2)}) collective-permute-start(bf16[2048,256]{1,0:T(8,128)(2,1)} %collective-permute-done.8.refs_1_.refs_2_), channel_id=1, source_target_pairs={{0,16},{16,0},{1,17},{17,1},{2,18},{18,2},{3,19},{19,3},{4,20},{20... | collective-permute-start | bytes 3145736 | tf_op jit(solution)/shard_map/ppermute | solution.py:244
  144.2 4.8 %collective-permute-start.17 = (bf16[256,2048]{1,0:T(8,128)(2,1)S(1)}, bf16[256,2048]{1,0:T(8,128)(2,1)}, u32[]{:S(2)}, u32[]{:S(2)}) collective-permute-start(bf16[256,2048]{1,0:T(8,128)(2,1)S(1)} %bitcast.31), channel_id=1, source_target_pairs={{0,8},{8,0},{1,9},{9,1},{2,10},{10,2},{3,11},{11,3},{4,12},{12,4},... | collective-permute-start | bytes 3145736 | tf_op jit(solution)/shard_map/ppermute | solution.py:50

commit v4 on v3

--- a/solution.py
+++ b/solution.py
@@ -39,11 +39,6 @@
             down = lax.ppermute(down, "z", shift(8, -1))
             blocks[step] = down
         yield blocks
-
-
-def replicate(value):
-    sent = jnp.broadcast_to(value[None], (8,) + value.shape)
-    return lax.all_to_all(sent, "z", 0, 0, tiled=True)
 
 
 def swap(value):
@@ -155,13 +150,15 @@
             acc = acc + f[:, g : g + 1] * ref[:, cols].astype(jnp.float32)
         for j in range(4):
             acc = acc + weights[j][:, g : g + 1] * suffix_values[j]
-        out_ref[:, cols] = acc.astype(jnp.bfloat16)
+        merged = acc.astype(jnp.bfloat16)
+        for copy in range(out_ref.shape[0]):
+            out_ref[copy, :, cols] = merged
 
 
 def combine(q, keys, values, lens, parts):
     return pl.pallas_call(
         combine_kernel,
-        out_shape=jax.ShapeDtypeStruct(q.shape, jnp.bfloat16),
+        out_shape=jax.ShapeDtypeStruct((8,) + q.shape, jnp.bfloat16),
         compiler_params=pltpu.CompilerParams(vmem_limit_bytes=VMEM_BYTES),
         name="combine",
     )(q, keys, values, lens, *parts)
@@ -243,7 +240,7 @@
 
     weight_uv = lax.ppermute(weight_u, "v", partner(2, 1))
 
-    own_rows = replicate(attended).reshape(-1, HEADS * HD)
+    own_rows = lax.all_to_all(attended, "z", 0, 0, tiled=True).reshape(-1, HEADS * HD)
     place = jnp.stack([lax.axis_index("c"), lax.axis_index(Y)]).astype(jnp.int32)
     terms = project(
         place, [own_rows, swap(own_rows)], [out_weight, weight_v, weight_u, weight_uv]

time: 191 us -> 191 us (level)
  no operation moved by 1% of the time
where the time goes in v4:
time: 191 us; the launch traced here: 190 us
  starting transfers between devices  79.8 us (42%)
  waiting for transfers between devices  49.2 us (26%)
  blocking collectives  35.8 us (19%)
  Pallas kernels  19.4 us (10%)
  local copies, waits for them, and re-layouts  3.22 us (2%)
    all_to_all x1, blocking collectives, per_device(): lax.all_to_all(terms.reshape(32, 2 * rows, cols), Y + HEAD, 0, 0, tiled=T...  35.8 us
    all_to_all x1, waiting for transfers between devices, per_device(): lax.all_to_all(attended, 'z', 0, 0, tiled=True).reshape(-1, HEADS * HD)  27.3 us
    ppermute x3, starting transfers between devices, ring(): down = lax.ppermute(down, 'z', shift(8, -1))  20.7 us
    pallas_call x4, Pallas kernels, attend(): pl.pallas_call(attention_kernel, out_shape=jax.ShapeDtypeStruct((rows, HE...  13.1 us
    ppermute x3, starting transfers between devices, swap(): return lax.ppermute(value, 'c', partner(2, 1))  12.7 us
    ppermute x4, waiting for transfers between devices, ring(): up = lax.ppermute(up, 'z', shift(8, 1))  10.9 us
    ppermute x3, starting transfers between devices, per_device(): parts[k] = message if k == 0 else lax.ppermute(message, Y, partner(4, k))  8.55 us
    all_to_all x1, starting transfers between devices, per_device(): own = lax.all_to_all(jnp.concatenate(split, axis=1), HEAD, 0, 0, tiled=True)  8.51 us
  transfers between devices with their start and end apart: 21, of which 7 were waited for; matrix products, arithmetic and copies ran while one was open for 1% of the time, Pallas kernels for 7%

profile of v4, /device:TPU:9, one launch (start us, length us, event | category | flops | bytes accessed | tf_op | source)
XLA Modules:
  0.0 189.8 jit_solution(4768728584904530675)
XLA Ops:
  0.0 0.0 copy-start
  0.0 0.8 copy-done
  0.8 0.9 bitcast_bitcast_fusion
  1.7 0.7 pad_maximum_fusion.1
  2.4 8.5 %all-to-all-start = ((bf16[8,64,128]{2,1,0:T(8,128)(2,1)}), bf16[8,64,128]{2,1,0:T(8,128)(2,1)S(1)}, u32[]{:S(2)}, u32[]{:S(2)}) async-start(bf16[8,64,128]{2,1,0:T(8,128)(2,1)} %pad_maximum_fusion.1), calls=%async_computation | async-start | bytes 262144 | tf_op jit(solution)/shard_map/all_to_all | solution.py:215
  10.9 2.4 %collective-permute-start.8 = (bf16[2048,256]{1,0:T(8,128)(2,1)}, bf16[2048,256]{1,0:T(8,128)(2,1)}, u32[]{:S(2)}, u32[]{:S(2)}) collective-permute-start(bf16[2048,256]{1,0:T(8,128)(2,1)} %refs_0_.1), channel_id=1, source_target_pairs={{0,32},{32,0},{1,33},{33,1},{2,34},{34,2},{3,35},{35,3},{4,36},{36... | collective-permute-start | bytes 3145736 | tf_op jit(solution)/shard_map/ppermute | solution.py:216
  13.3 3.0 %collective-permute-start.9 = (bf16[2048,256]{1,0:T(8,128)(2,1)}, bf16[2048,256]{1,0:T(8,128)(2,1)S(1)}, u32[]{:S(2)}, u32[]{:S(2)}) collective-permute-start(bf16[2048,256]{1,0:T(8,128)(2,1)} %refs_0_.1), channel_id=1, source_target_pairs={{0,16},{16,0},{1,17},{17,1},{2,18},{18,2},{3,19},{19,3},{4,20},{20... | collective-permute-start | bytes 3145736 | tf_op jit(solution)/shard_map/ppermute | solution.py:217
  16.3 4.9 %all-to-all-done = bf16[8,64,128]{2,1,0:T(8,128)(2,1)S(1)} async-done(((bf16[8,64,128]{2,1,0:T(8,128)(2,1)}), bf16[8,64,128]{2,1,0:T(8,128)(2,1)S(1)}, u32[]{:S(2)}, u32[]{:S(2)}) %all-to-all-start) | async-done | bytes 131104 | tf_op jit(solution)/shard_map/all_to_all | solution.py:215
  21.1 10.7 %collective-permute-start.1 = (bf16[8,64,128]{2,1,0:T(8,128)(2,1)S(1)}, bf16[8,64,128]{2,1,0:T(8,128)(2,1)S(1)}, u32[]{:S(2)}, u32[]{:S(2)}) collective-permute-start(bf16[8,64,128]{2,1,0:T(8,128)(2,1)S(1)} %all-to-all-done), channel_id=1, source_target_pairs={{0,448},{64,0},{128,64},{192,128},{256,192},{320,256},{384,320},{4... | collective-permute-start | bytes 393224 | tf_op jit(solution)/shard_map/ppermute | solution.py:39
  31.8 1.9 %collective-permute-start = (bf16[8,64,128]{2,1,0:T(8,128)(2,1)S(1)}, bf16[8,64,128]{2,1,0:T(8,128)(2,1)S(1)}, u32[]{:S(2)}, u32[]{:S(2)}) collective-permute-start(bf16[8,64,128]{2,1,0:T(8,128)(2,1)S(1)} %all-to-all-done), channel_id=1, source_target_pairs={{0,64},{64,128},{128,192},{192,256},{256,320},{320,384},{384,448},... | collective-permute-start | bytes 393224 | tf_op jit(solution)/shard_map/ppermute | solution.py:36
  33.8 0.0 collective-permute-done.1
  33.8 5.2 %collective-permute-start.3 = (bf16[8,64,128]{2,1,0:T(8,128)(2,1)S(1)}, bf16[8,64,128]{2,1,0:T(8,128)(2,1)S(1)}, u32[]{:S(2)}, u32[]{:S(2)}) collective-permute-start(bf16[8,64,128]{2,1,0:T(8,128)(2,1)S(1)} %collective-permute-done.1), channel_id=1, source_target_pairs={{0,448},{64,0},{128,64},{192,128},{256,192},{320,256},{384,320},{4... | collective-permute-start | bytes 393224 | tf_op jit(solution)/shard_map/ppermute | solution.py:39
  39.0 0.0 collective-permute-done
  39.0 1.9 %collective-permute-start.2 = (bf16[8,64,128]{2,1,0:T(8,128)(2,1)S(1)}, bf16[8,64,128]{2,1,0:T(8,128)(2,1)S(1)}, u32[]{:S(2)}, u32[]{:S(2)}) collective-permute-start(bf16[8,64,128]{2,1,0:T(8,128)(2,1)S(1)} %collective-permute-done), channel_id=1, source_target_pairs={{0,64},{64,128},{128,192},{192,256},{256,320},{320,384},{384,448},... | collective-permute-start | bytes 393224 | tf_op jit(solution)/shard_map/ppermute | solution.py:36
  41.0 4.9 %collective-permute-done.2 = bf16[8,64,128]{2,1,0:T(8,128)(2,1)S(1)} collective-permute-done((bf16[8,64,128]{2,1,0:T(8,128)(2,1)S(1)}, bf16[8,64,128]{2,1,0:T(8,128)(2,1)S(1)}, u32[]{:S(2)}, u32[]{:S(2)}) %collective-permute-start.2) | collective-permute-done | bytes 131104 | tf_op jit(solution)/shard_map/ppermute | solution.py:36
  45.9 1.9 %collective-permute-start.5 = (bf16[8,64,128]{2,1,0:T(8,128)(2,1)S(1)}, bf16[8,64,128]{2,1,0:T(8,128)(2,1)S(1)}, u32[]{:S(2)}, u32[]{:S(2)}) collective-permute-start(bf16[8,64,128]{2,1,0:T(8,128)(2,1)S(1)} %collective-permute-done.2), channel_id=1, source_target_pairs={{0,64},{64,128},{128,192},{192,256},{256,320},{320,384},{384,448},... | collective-permute-start | bytes 393224 | tf_op jit(solution)/shard_map/ppermute | solution.py:36
  47.8 0.0 copy-start.4
  47.9 0.0 collective-permute-done.3
  47.9 0.0 copy-start.7
  47.9 6.5 %collective-permute-start.4 = (bf16[40,64,128]{2,1,0:T(8,128)(2,1)S(1)}, bf16[40,64,128]{2,1,0:T(8,128)(2,1)S(1)}, u32[]{:S(2)}, u32[]{:S(2)}) collective-permute-start(bf16[40,64,128]{2,1,0:T(8,128)(2,1)S(1)} %constant_dynamic-update-slice_fusion.refs_0_), channel_id=1, source_target_pairs={{0,8},{8,0},{1,9},{9,1},{2,10},{10,2},{3,11},{11,3},{4,12},{12,4},... | collective-permute-start | bytes 1966088 | tf_op jit(solution)/shard_map/ppermute | solution.py:45
  54.4 4.9 %collective-permute-start.6 = (bf16[8,64,128]{2,1,0:T(8,128)(2,1)S(1)}, bf16[8,64,128]{2,1,0:T(8,128)(2,1)S(1)}, u32[]{:S(2)}, u32[]{:S(2)}) collective-permute-start(bf16[8,64,128]{2,1,0:T(8,128)(2,1)S(1)} %collective-permute-done.3), channel_id=1, source_target_pairs={{0,448},{64,0},{128,64},{192,128},{256,192},{320,256},{384,320},{4... | collective-permute-start | bytes 393224 | tf_op jit(solution)/shard_map/ppermute | solution.py:39
  59.3 0.0 collective-permute-done.5
  59.3 1.9 %collective-permute-start.7 = (bf16[8,64,128]{2,1,0:T(8,128)(2,1)S(1)}, bf16[8,64,128]{2,1,0:T(8,128)(2,1)S(1)}, u32[]{:S(2)}, u32[]{:S(2)}) collective-permute-start(bf16[8,64,128]{2,1,0:T(8,128)(2,1)S(1)} %collective-permute-done.5), channel_id=1, source_target_pairs={{0,64},{64,128},{128,192},{192,256},{256,320},{320,384},{384,448},... | collective-permute-start | bytes 393224 | tf_op jit(solution)/shard_map/ppermute | solution.py:36
  61.2 5.9 %collective-permute-done.7.refs_0_ = bf16[8,64,128]{2,1,0:T(8,128)(2,1)S(1)} collective-permute-done((bf16[8,64,128]{2,1,0:T(8,128)(2,1)S(1)}, bf16[8,64,128]{2,1,0:T(8,128)(2,1)S(1)}, u32[]{:S(2)}, u32[]{:S(2)}) %collective-permute-start.7) | collective-permute-done | bytes 131104 | tf_op jit(solution)/shard_map/ppermute | solution.py:36
  67.2 2.3 %collective-permute-start.15 = (bf16[32,2048]{1,0:T(8,128)(2,1)S(1)}, bf16[32,2048]{1,0:T(8,128)(2,1)S(1)}, u32[]{:S(2)}, u32[]{:S(2)}) collective-permute-start(bf16[32,2048]{1,0:T(8,128)(2,1)S(1)} %bitcast.34), channel_id=1, source_target_pairs={{0,48},{16,32},{32,16},{48,0},{1,49},{17,33},{33,17},{49,1},{2,50}... | collective-permute-start | bytes 393224 | tf_op jit(solution)/shard_map/ppermute | solution.py:210
  69.4 0.0 collective-permute-done.8.refs_1_.refs_2_
  69.5 3.9 %collective-permute-start.13 = (bf16[32,2048]{1,0:T(8,128)(2,1)S(1)}, bf16[32,2048]{1,0:T(8,128)(2,1)}, u32[]{:S(2)}, u32[]{:S(2)}) collective-permute-start(bf16[32,2048]{1,0:T(8,128)(2,1)S(1)} %bitcast.35), channel_id=1, source_target_pairs={{0,32},{16,48},{32,0},{48,16},{1,33},{17,49},{33,1},{49,17},{2,34}... | collective-permute-start | bytes 393224 | tf_op jit(solution)/shard_map/ppermute | solution.py:210
  73.4 0.0 collective-permute-done.9.refs_2_.refs_1_
  73.4 2.2 %collective-permute-start.11 = (bf16[32,2048]{1,0:T(8,128)(2,1)S(1)}, bf16[32,2048]{1,0:T(8,128)(2,1)}, u32[]{:S(2)}, u32[]{:S(2)}) collective-permute-start(bf16[32,2048]{1,0:T(8,128)(2,1)S(1)} %bitcast.36), channel_id=1, source_target_pairs={{0,16},{16,0},{32,48},{48,32},{1,17},{17,1},{33,49},{49,33},{2,18}... | collective-permute-start | bytes 393224 | tf_op jit(solution)/shard_map/ppermute | solution.py:210
  75.6 0.0 collective-permute-done.6
  75.6 1.0 pad_maximum_fusion.refs_2_
  76.6 3.9 %collective-permute-start.10 = (bf16[24,64,128]{2,1,0:T(8,128)(2,1)S(1)}, bf16[24,64,128]{2,1,0:T(8,128)(2,1)S(1)}, u32[]{:S(2)}, u32[]{:S(2)}) collective-permute-start(bf16[24,64,128]{2,1,0:T(8,128)(2,1)S(1)} %pad_maximum_fusion.refs_2_), channel_id=1, source_target_pairs={{0,8},{8,0},{1,9},{9,1},{2,10},{10,2},{3,11},{11,3},{4,12},{12,4},... | collective-permute-start | bytes 1179656 | tf_op jit(solution)/shard_map/ppermute | solution.py:45
  80.5 0.0 collective-permute-done.11.q_ref
  80.5 0.0 collective-permute-done.4.refs_1_
  80.5 1.3 collective-permute-done.10.refs_3_
  81.8 3.7 %attend.5 = bf16[32,2176]{1,0:T(8,128)(2,1)S(1)} custom-call(bf16[32,2048]{1,0:T(8,128)(2,1)} %collective-permute-done.11.q_ref, bf16[40,64,128]{2,1,0:T(8,128)(2,1)S(1)} %constant_dynamic-update-slice_fusion.refs_0_, bf16[40,64,128]{2,1,0:T(8,128)(2,1)S(1)} %collective-permute-done.4.refs_1_, bf16[24,64,128]{2,1,0:T(8,128)(2,1)S(1)} %pad_maximum_fusion.refs_2_, ...), custom_call_target="tpu_custom_call" | custom-call | tf_op jit(solution)/shard_map/attend/pallas_call | solution.py:104
  85.5 3.1 %collective-permute-start.12 = (bf16[32,2176]{1,0:T(8,128)(2,1)S(1)}, bf16[32,2176]{1,0:T(8,128)(2,1)S(1)}, u32[]{:S(2)}, u32[]{:S(2)}) collective-permute-start(bf16[32,2176]{1,0:T(8,128)(2,1)S(1)} %attend.5), channel_id=1, source_target_pairs={{0,16},{16,0},{32,48},{48,32},{1,17},{17,1},{33,49},{49,33},{2,18}... | collective-permute-start | bytes 417800 | tf_op jit(solution)/shard_map/ppermute | solution.py:231
  88.6 0.0 collective-permute-done.13.q_ref
  88.6 3.7 %attend.6 = bf16[32,2176]{1,0:T(8,128)(2,1)S(1)} custom-call(bf16[32,2048]{1,0:T(8,128)(2,1)} %collective-permute-done.13.q_ref, bf16[40,64,128]{2,1,0:T(8,128)(2,1)S(1)} %constant_dynamic-update-slice_fusion.refs_0_, bf16[40,64,128]{2,1,0:T(8,128)(2,1)S(1)} %collective-permute-done.4.refs_1_, bf16[24,64,128]{2,1,0:T(8,128)(2,1)S(1)} %pad_maximum_fusion.refs_2_, ...), custom_call_target="tpu_custom_call" | custom-call | tf_op jit(solution)/shard_map/attend/pallas_call | solution.py:104
  92.3 2.3 %collective-permute-start.14 = (bf16[32,2176]{1,0:T(8,128)(2,1)S(1)}, bf16[32,2176]{1,0:T(8,128)(2,1)S(1)}, u32[]{:S(2)}, u32[]{:S(2)}) collective-permute-start(bf16[32,2176]{1,0:T(8,128)(2,1)S(1)} %attend.6), channel_id=1, source_target_pairs={{0,32},{16,48},{32,0},{48,16},{1,33},{17,49},{33,1},{49,17},{2,34}... | collective-permute-start | bytes 417800 | tf_op jit(solution)/shard_map/ppermute | solution.py:231
  94.6 0.0 collective-permute-done.15.q_ref
  94.7 0.0 copy-start.8
  94.7 0.0 copy-start.10
  94.7 2.8 %attend.7 = bf16[32,2176]{1,0:T(8,128)(2,1)S(1)} custom-call(bf16[32,2048]{1,0:T(8,128)(2,1)S(1)} %collective-permute-done.15.q_ref, bf16[40,64,128]{2,1,0:T(8,128)(2,1)S(1)} %constant_dynamic-update-slice_fusion.refs_0_, bf16[40,64,128]{2,1,0:T(8,128)(2,1)S(1)} %collective-permute-done.4.refs_1_, bf16[24,64,128]{2,1,0:T(8,128)(2,1)S(1)} %pad_maximum_fusion.refs_2_, ...), custom_call_target="tpu_custom_call" | custom-call | tf_op jit(solution)/shard_map/attend/pallas_call | solution.py:104
  97.5 3.2 %collective-permute-start.16 = (bf16[32,2176]{1,0:T(8,128)(2,1)S(1)}, bf16[32,2176]{1,0:T(8,128)(2,1)S(1)}, u32[]{:S(2)}, u32[]{:S(2)}) collective-permute-start(bf16[32,2176]{1,0:T(8,128)(2,1)S(1)} %attend.7), channel_id=1, source_target_pairs={{0,48},{16,32},{32,16},{48,0},{1,49},{17,33},{33,17},{49,1},{2,50}... | collective-permute-start | bytes 417800 | tf_op jit(solution)/shard_map/ppermute | solution.py:231
  100.7 0.0 copy-start.9
  100.8 0.1 copy.36.len_ref
  100.8 0.6 copy-done.9
  101.4 2.8 %attend.4.m0_ref = bf16[32,2176]{1,0:T(8,128)(2,1)S(1)} custom-call(bf16[32,2048]{1,0:T(8,128)(2,1)S(1)} %bitcast.37, bf16[40,64,128]{2,1,0:T(8,128)(2,1)S(1)} %constant_dynamic-update-slice_fusion.refs_0_, bf16[40,64,128]{2,1,0:T(8,128)(2,1)S(1)} %collective-permute-done.4.refs_1_, bf16[24,64,128]{2,1,0:T(8,128)(2,1)S(1)} %pad_maximum_fusion.refs_2_, ...), custom_call_target="tpu_custom_call" | custom-call | tf_op jit(solution)/shard_map/attend/pallas_call | solution.py:104
  104.3 0.0 collective-permute-done.12.m1_ref
  104.3 0.0 collective-permute-done.14.m2_ref
  104.3 2.5 %collective-permute-done.16.m3_ref = bf16[32,2176]{1,0:T(8,128)(2,1)S(1)} collective-permute-done((bf16[32,2176]{1,0:T(8,128)(2,1)S(1)}, bf16[32,2176]{1,0:T(8,128)(2,1)S(1)}, u32[]{:S(2)}, u32[]{:S(2)}) %collective-permute-start.16) | collective-permute-done | bytes 139296 | tf_op jit(solution)/shard_map/ppermute | solution.py:231
  106.8 2.1 %combine.1 = bf16[8,32,2048]{2,1,0:T(8,128)(2,1)} custom-call(bf16[32,2048]{1,0:T(8,128)(2,1)S(1)} %bitcast.38, f32[4,16,128]{2,1,0:T(8,128)S(1)} %maximum_convert_fusion.k_ref, f32[4,16,128]{2,1,0:T(8,128)S(1)} %maximum_convert_fusion.1.v_ref, s32[16,1]{1,0:T(8,128)S(1)} %copy.36.len_ref, bf16[32,2176]{1,0:T(8,128)(2,1)S(1)} %attend.4.m0_ref, ...), custom_call_target="tpu_custom_call" | custom-call | tf_op jit(solution)/shard_map/combine/pallas_call | solution.py:159
  108.9 6.0 %all-to-all-start.1 = ((bf16[8,32,2048]{2,1,0:T(8,128)(2,1)}), bf16[8,32,2048]{2,1,0:T(8,128)(2,1)S(1)}, u32[]{:S(2)}, u32[]{:S(2)}) async-start(bf16[8,32,2048]{2,1,0:T(8,128)(2,1)} %combine.1), calls=%async_computation.1 | async-start | bytes 2097152 | tf_op jit(solution)/shard_map/all_to_all | solution.py:243
  114.9 1.9 %collective-permute-start.18 = (bf16[2048,256]{1,0:T(8,128)(2,1)}, bf16[2048,256]{1,0:T(8,128)(2,1)}, u32[]{:S(2)}, u32[]{:S(2)}) collective-permute-start(bf16[2048,256]{1,0:T(8,128)(2,1)} %collective-permute-done.8.refs_1_.refs_2_), channel_id=1, source_target_pairs={{0,16},{16,0},{1,17},{17,1},{2,18},{18,2},{3,19},{19,3},{4,20},{20... | collective-permute-start | bytes 3145736 | tf_op jit(solution)/shard_map/ppermute | solution.py:241
  116.8 27.3 %all-to-all-done.1 = bf16[8,32,2048]{2,1,0:T(8,128)(2,1)S(1)} async-done(((bf16[8,32,2048]{2,1,0:T(8,128)(2,1)}), bf16[8,32,2048]{2,1,0:T(8,128)(2,1)S(1)}, u32[]{:S(2)}, u32[]{:S(2)}) %all-to-all-start.1) | async-done | bytes 1048608 | tf_op jit(solution)/shard_map/all_to_all | solution.py:243
  144.1 2.4 %collective-permute-start.17 = (bf16[256,2048]{1,0:T(8,128)(2,1)S(1)}, bf16[256,2048]{1,0:T(8,128)(2,1)}, u32[]{:S(2)}, u32[]{:S(2)}) collective-permute-start(bf16[256,2048]{1,0:T(8,128)(2,1)S(1)} %bitcast.31), channel_id=1, source_target_pairs={{0,8},{8,0},{1,9},{9,1},{2,10},{10,2},{3,11},{11,3},{4,12},{12,4},... | collective-permute-start | bytes 3145736 | tf_op jit(solution)/shard_map/ppermute | solution.py:45
  146.5 0.1 pad_add_fusion.place_ref
  146.6 0.0 collective-permute-done.18.refs_3_
  146.6 2.3 %collective-permute-done.17.other_ref = bf16[256,2048]{1,0:T(8,128)(2,1)} collective-permute-done((bf16[256,2048]{1,0:T(8,128)(2,1)S(1)}, bf16[256,2048]{1,0:T(8,128)(2,1)}, u32[]{:S(2)}, u32[]{:S(2)}) %collective-permute-start.17) | collective-permute-done | bytes 1048608 | tf_op jit(solution)/shard_map/ppermute | solution.py:45
  148.9 4.2 %project.1 = bf16[4,8,2,32,256]{4,3,2,1,0:T(8,128)(2,1)S(1)} custom-call(s32[2]{0:T(128)S(1)} %pad_add_fusion.place_ref, bf16[256,2048]{1,0:T(8,128)(2,1)S(1)} %bitcast.32, bf16[256,2048]{1,0:T(8,128)(2,1)} %collective-permute-done.17.other_ref, bf16[2048,256]{1,0:T(8,128)(2,1)S(1)} %copy-done.3, bf16[2048,256]{1,0:T(8,128)(2,1)S(1)} %copy-done.2, ...), custom_call_target="tpu_custom_call" | custom-call | tf_op jit(solution)/shard_map/project/pallas_call | solution.py:185
  153.1 35.8 %all_to_all.15 = bf16[32,64,256]{2,1,0:T(8,128)(2,1)S(1)} all-to-all(bf16[32,64,256]{2,1,0:T(8,128)(2,1)S(1)} %bitcast.33), channel_id=1, replica_groups=mesh['z'=8,'u'=2,'v'=2,'c'=2,'x'=4,'w'=2] {'u','v','x','w'}, dimensions={0} | all-to-all | bytes 2097152 | tf_op jit(solution)/shard_map/all_to_all | solution.py:250
  188.9 0.2 reduce_sum.12
  189.1 0.7 copy.37
  (26 shorter events, 0.2 us)
Async XLA Ops:
  0.0 0.8 copy-start
  2.4 31.4 %copy-start.6 = (bf16[16,2,128]{2,1,0:T(2,128)(2,1)S(1)}, bf16[16,2,128]{2,1,0:T(2,128)(2,1)}, u32[]{:S(2)}) copy-start(bf16[16,2,128]{2,1,0:T(2,128)(2,1)} %param.12) | copy-start | bytes 24580
  2.4 18.8 %all-to-all-start = ((bf16[8,64,128]{2,1,0:T(8,128)(2,1)}), bf16[8,64,128]{2,1,0:T(8,128)(2,1)S(1)}, u32[]{:S(2)}, u32[]{:S(2)}) async-start(bf16[8,64,128]{2,1,0:T(8,128)(2,1)} %pad_maximum_fusion.1), calls=%async_computation | async-start | bytes 262144 | tf_op jit(solution)/shard_map/all_to_all | solution.py:215
  10.9 58.6 %collective-permute-start.8 = (bf16[2048,256]{1,0:T(8,128)(2,1)}, bf16[2048,256]{1,0:T(8,128)(2,1)}, u32[]{:S(2)}, u32[]{:S(2)}) collective-permute-start(bf16[2048,256]{1,0:T(8,128)(2,1)} %refs_0_.1), channel_id=1, source_target_pairs={{0,32},{32,0},{1,33},{33,1},{2,34},{34,2},{3,35},{35,3},{4,36},{36... | collective-permute-start | bytes 3145736 | tf_op jit(solution)/shard_map/ppermute | solution.py:216
  13.3 60.1 %collective-permute-start.9 = (bf16[2048,256]{1,0:T(8,128)(2,1)}, bf16[2048,256]{1,0:T(8,128)(2,1)S(1)}, u32[]{:S(2)}, u32[]{:S(2)}) collective-permute-start(bf16[2048,256]{1,0:T(8,128)(2,1)} %refs_0_.1), channel_id=1, source_target_pairs={{0,16},{16,0},{1,17},{17,1},{2,18},{18,2},{3,19},{19,3},{4,20},{20... | collective-permute-start | bytes 3145736 | tf_op jit(solution)/shard_map/ppermute | solution.py:217
  21.1 12.6 %collective-permute-start.1 = (bf16[8,64,128]{2,1,0:T(8,128)(2,1)S(1)}, bf16[8,64,128]{2,1,0:T(8,128)(2,1)S(1)}, u32[]{:S(2)}, u32[]{:S(2)}) collective-permute-start(bf16[8,64,128]{2,1,0:T(8,128)(2,1)S(1)} %all-to-all-done), channel_id=1, source_target_pairs={{0,448},{64,0},{128,64},{192,128},{256,192},{320,256},{384,320},{4... | collective-permute-start | bytes 393224 | tf_op jit(solution)/shard_map/ppermute | solution.py:39
  31.8 7.2 %collective-permute-start = (bf16[8,64,128]{2,1,0:T(8,128)(2,1)S(1)}, bf16[8,64,128]{2,1,0:T(8,128)(2,1)S(1)}, u32[]{:S(2)}, u32[]{:S(2)}) collective-permute-start(bf16[8,64,128]{2,1,0:T(8,128)(2,1)S(1)} %all-to-all-done), channel_id=1, source_target_pairs={{0,64},{64,128},{128,192},{192,256},{256,320},{320,384},{384,448},... | collective-permute-start | bytes 393224 | tf_op jit(solution)/shard_map/ppermute | solution.py:36
  33.8 14.1 %collective-permute-start.3 = (bf16[8,64,128]{2,1,0:T(8,128)(2,1)S(1)}, bf16[8,64,128]{2,1,0:T(8,128)(2,1)S(1)}, u32[]{:S(2)}, u32[]{:S(2)}) collective-permute-start(bf16[8,64,128]{2,1,0:T(8,128)(2,1)S(1)} %collective-permute-done.1), channel_id=1, source_target_pairs={{0,448},{64,0},{128,64},{192,128},{256,192},{320,256},{384,320},{4... | collective-permute-start | bytes 393224 | tf_op jit(solution)/shard_map/ppermute | solution.py:39
  39.0 6.9 %collective-permute-start.2 = (bf16[8,64,128]{2,1,0:T(8,128)(2,1)S(1)}, bf16[8,64,128]{2,1,0:T(8,128)(2,1)S(1)}, u32[]{:S(2)}, u32[]{:S(2)}) collective-permute-start(bf16[8,64,128]{2,1,0:T(8,128)(2,1)S(1)} %collective-permute-done), channel_id=1, source_target_pairs={{0,64},{64,128},{128,192},{192,256},{256,320},{320,384},{384,448},... | collective-permute-start | bytes 393224 | tf_op jit(solution)/shard_map/ppermute | solution.py:36
  45.9 13.4 %collective-permute-start.5 = (bf16[8,64,128]{2,1,0:T(8,128)(2,1)S(1)}, bf16[8,64,128]{2,1,0:T(8,128)(2,1)S(1)}, u32[]{:S(2)}, u32[]{:S(2)}) collective-permute-start(bf16[8,64,128]{2,1,0:T(8,128)(2,1)S(1)} %collective-permute-done.2), channel_id=1, source_target_pairs={{0,64},{64,128},{128,192},{192,256},{256,320},{320,384},{384,448},... | collective-permute-start | bytes 393224 | tf_op jit(solution)/shard_map/ppermute | solution.py:36
  47.8 19.3 %copy-start.4 = (bf16[2,16,2048]{2,1,0:T(8,128)(2,1)S(1)}, bf16[2,16,2048]{2,1,0:T(8,128)(2,1)}, u32[]{:S(2)}) copy-start(bf16[2,16,2048]{2,1,0:T(8,128)(2,1)} %param.9) | copy-start | bytes 393220
  47.9 13.3 %copy-start.7 = (bf16[16,2,128]{2,1,0:T(2,128)(2,1)S(1)}, bf16[16,2,128]{2,1,0:T(2,128)(2,1)}, u32[]{:S(2)}) copy-start(bf16[16,2,128]{2,1,0:T(2,128)(2,1)} %param.13) | copy-start | bytes 24580
  47.9 32.6 %collective-permute-start.4 = (bf16[40,64,128]{2,1,0:T(8,128)(2,1)S(1)}, bf16[40,64,128]{2,1,0:T(8,128)(2,1)S(1)}, u32[]{:S(2)}, u32[]{:S(2)}) collective-permute-start(bf16[40,64,128]{2,1,0:T(8,128)(2,1)S(1)} %constant_dynamic-update-slice_fusion.refs_0_), channel_id=1, source_target_pairs={{0,8},{8,0},{1,9},{9,1},{2,10},{10,2},{3,11},{11,3},{4,12},{12,4},... | collective-permute-start | bytes 1966088 | tf_op jit(solution)/shard_map/ppermute | solution.py:45
  54.4 21.2 %collective-permute-start.6 = (bf16[8,64,128]{2,1,0:T(8,128)(2,1)S(1)}, bf16[8,64,128]{2,1,0:T(8,128)(2,1)S(1)}, u32[]{:S(2)}, u32[]{:S(2)}) collective-permute-start(bf16[8,64,128]{2,1,0:T(8,128)(2,1)S(1)} %collective-permute-done.3), channel_id=1, source_target_pairs={{0,448},{64,0},{128,64},{192,128},{256,192},{320,256},{384,320},{4... | collective-permute-start | bytes 393224 | tf_op jit(solution)/shard_map/ppermute | solution.py:39
  59.3 7.9 %collective-permute-start.7 = (bf16[8,64,128]{2,1,0:T(8,128)(2,1)S(1)}, bf16[8,64,128]{2,1,0:T(8,128)(2,1)S(1)}, u32[]{:S(2)}, u32[]{:S(2)}) collective-permute-start(bf16[8,64,128]{2,1,0:T(8,128)(2,1)S(1)} %collective-permute-done.5), channel_id=1, source_target_pairs={{0,64},{64,128},{128,192},{192,256},{256,320},{320,384},{384,448},... | collective-permute-start | bytes 393224 | tf_op jit(solution)/shard_map/ppermute | solution.py:36
  67.2 8.4 %copy-start.5 = (bf16[8,64,128]{2,1,0:T(8,128)(2,1)}, bf16[8,64,128]{2,1,0:T(8,128)(2,1)S(1)}, u32[]{:S(2)}) copy-start(bf16[8,64,128]{2,1,0:T(8,128)(2,1)S(1)} %collective-permute-done.7.refs_0_) | copy-start | bytes 393220
  67.2 27.5 %collective-permute-start.15 = (bf16[32,2048]{1,0:T(8,128)(2,1)S(1)}, bf16[32,2048]{1,0:T(8,128)(2,1)S(1)}, u32[]{:S(2)}, u32[]{:S(2)}) collective-permute-start(bf16[32,2048]{1,0:T(8,128)(2,1)S(1)} %bitcast.34), channel_id=1, source_target_pairs={{0,48},{16,32},{32,16},{48,0},{1,49},{17,33},{33,17},{49,1},{2,50}... | collective-permute-start | bytes 393224 | tf_op jit(solution)/shard_map/ppermute | solution.py:210
  69.5 19.2 %collective-permute-start.13 = (bf16[32,2048]{1,0:T(8,128)(2,1)S(1)}, bf16[32,2048]{1,0:T(8,128)(2,1)}, u32[]{:S(2)}, u32[]{:S(2)}) collective-permute-start(bf16[32,2048]{1,0:T(8,128)(2,1)S(1)} %bitcast.35), channel_id=1, source_target_pairs={{0,32},{16,48},{32,0},{48,16},{1,33},{17,49},{33,1},{49,17},{2,34}... | collective-permute-start | bytes 393224 | tf_op jit(solution)/shard_map/ppermute | solution.py:210
  73.4 2.2 %copy-start.1 = (bf16[2048,256]{1,0:T(8,128)(2,1)}, bf16[2048,256]{1,0:T(8,128)(2,1)S(1)}, u32[]{:S(2)}) copy-start(bf16[2048,256]{1,0:T(8,128)(2,1)S(1)} %collective-permute-done.9.refs_2_.refs_1_) | copy-start | bytes 3145732
  73.4 7.1 %collective-permute-start.11 = (bf16[32,2048]{1,0:T(8,128)(2,1)S(1)}, bf16[32,2048]{1,0:T(8,128)(2,1)}, u32[]{:S(2)}, u32[]{:S(2)}) collective-permute-start(bf16[32,2048]{1,0:T(8,128)(2,1)S(1)} %bitcast.36), channel_id=1, source_target_pairs={{0,16},{16,0},{32,48},{48,32},{1,17},{17,1},{33,49},{49,33},{2,18}... | collective-permute-start | bytes 393224 | tf_op jit(solution)/shard_map/ppermute | solution.py:210
  76.6 5.2 %collective-permute-start.10 = (bf16[24,64,128]{2,1,0:T(8,128)(2,1)S(1)}, bf16[24,64,128]{2,1,0:T(8,128)(2,1)S(1)}, u32[]{:S(2)}, u32[]{:S(2)}) collective-permute-start(bf16[24,64,128]{2,1,0:T(8,128)(2,1)S(1)} %pad_maximum_fusion.refs_2_), channel_id=1, source_target_pairs={{0,8},{8,0},{1,9},{9,1},{2,10},{10,2},{3,11},{11,3},{4,12},{12,4},... | collective-permute-start | bytes 1179656 | tf_op jit(solution)/shard_map/ppermute | solution.py:45
  85.5 18.8 %collective-permute-start.12 = (bf16[32,2176]{1,0:T(8,128)(2,1)S(1)}, bf16[32,2176]{1,0:T(8,128)(2,1)S(1)}, u32[]{:S(2)}, u32[]{:S(2)}) collective-permute-start(bf16[32,2176]{1,0:T(8,128)(2,1)S(1)} %attend.5), channel_id=1, source_target_pairs={{0,16},{16,0},{32,48},{48,32},{1,17},{17,1},{33,49},{49,33},{2,18}... | collective-permute-start | bytes 417800 | tf_op jit(solution)/shard_map/ppermute | solution.py:231
  92.3 11.9 %collective-permute-start.14 = (bf16[32,2176]{1,0:T(8,128)(2,1)S(1)}, bf16[32,2176]{1,0:T(8,128)(2,1)S(1)}, u32[]{:S(2)}, u32[]{:S(2)}) collective-permute-start(bf16[32,2176]{1,0:T(8,128)(2,1)S(1)} %attend.6), channel_id=1, source_target_pairs={{0,32},{16,48},{32,0},{48,16},{1,33},{17,49},{33,1},{49,17},{2,34}... | collective-permute-start | bytes 417800 | tf_op jit(solution)/shard_map/ppermute | solution.py:231
  94.7 6.1 %copy-start.8 = (bf16[2,16,128]{2,1,0:T(8,128)(2,1)S(1)}, bf16[2,16,128]{2,1,0:T(8,128)(2,1)}, u32[]{:S(2)}) copy-start(bf16[2,16,128]{2,1,0:T(8,128)(2,1)} %param.15) | copy-start | bytes 24580
  94.7 6.1 %copy-start.10 = (s32[16]{0:T(128)S(1)}, s32[16]{0:T(128)}, u32[]{:S(2)}) copy-start(s32[16]{0:T(128)} %param.16) | copy-start | bytes 196
  97.5 9.3 %collective-permute-start.16 = (bf16[32,2176]{1,0:T(8,128)(2,1)S(1)}, bf16[32,2176]{1,0:T(8,128)(2,1)S(1)}, u32[]{:S(2)}, u32[]{:S(2)}) collective-permute-start(bf16[32,2176]{1,0:T(8,128)(2,1)S(1)} %attend.7), channel_id=1, source_target_pairs={{0,48},{16,32},{32,16},{48,0},{1,49},{17,33},{33,17},{49,1},{2,50}... | collective-permute-start | bytes 417800 | tf_op jit(solution)/shard_map/ppermute | solution.py:231
  100.7 0.7 copy-start.9
  108.9 40.0 %copy-start.2 = (bf16[2048,256]{1,0:T(8,128)(2,1)S(1)}, bf16[2048,256]{1,0:T(8,128)(2,1)}, u32[]{:S(2)}) copy-start(bf16[2048,256]{1,0:T(8,128)(2,1)} %copy-done.1) | copy-start | bytes 3145732
  108.9 40.0 %copy-start.3 = (bf16[2048,256]{1,0:T(8,128)(2,1)S(1)}, bf16[2048,256]{1,0:T(8,128)(2,1)}, u32[]{:S(2)}) copy-start(bf16[2048,256]{1,0:T(8,128)(2,1)} %refs_0_.1) | copy-start | bytes 3145732
  108.9 35.2 %all-to-all-start.1 = ((bf16[8,32,2048]{2,1,0:T(8,128)(2,1)}), bf16[8,32,2048]{2,1,0:T(8,128)(2,1)S(1)}, u32[]{:S(2)}, u32[]{:S(2)}) async-start(bf16[8,32,2048]{2,1,0:T(8,128)(2,1)} %combine.1), calls=%async_computation.1 | async-start | bytes 2097152 | tf_op jit(solution)/shard_map/all_to_all | solution.py:243
  114.9 31.7 %collective-permute-start.18 = (bf16[2048,256]{1,0:T(8,128)(2,1)}, bf16[2048,256]{1,0:T(8,128)(2,1)}, u32[]{:S(2)}, u32[]{:S(2)}) collective-permute-start(bf16[2048,256]{1,0:T(8,128)(2,1)} %collective-permute-done.8.refs_1_.refs_2_), channel_id=1, source_target_pairs={{0,16},{16,0},{1,17},{17,1},{2,18},{18,2},{3,19},{19,3},{4,20},{20... | collective-permute-start | bytes 3145736 | tf_op jit(solution)/shard_map/ppermute | solution.py:241
  144.1 4.8 %collective-permute-start.17 = (bf16[256,2048]{1,0:T(8,128)(2,1)S(1)}, bf16[256,2048]{1,0:T(8,128)(2,1)}, u32[]{:S(2)}, u32[]{:S(2)}) collective-permute-start(bf16[256,2048]{1,0:T(8,128)(2,1)S(1)} %bitcast.31), channel_id=1, source_target_pairs={{0,8},{8,0},{1,9},{9,1},{2,10},{10,2},{3,11},{11,3},{4,12},{12,4},... | collective-permute-start | bytes 3145736 | tf_op jit(solution)/shard_map/ppermute | solution.py:45
